TPU v7x, 128 devices: a whole 4x4x4 slice. The times are simulated.
128 devices in a mesh: line: 32 (over x, y, core), tm: 4 (over z).
Axes of the slice: x: 4, y: 4, z: 4, core: 2. Of those that a mesh axis runs over, the one named last changes fastest.
Arguments:
- gust_coef: bfloat16 [128, 128, 32, 256], P(('line', 'tm')), may hold values from -0.625 to 0.625
- mean_wind: float32 [32, 256], P('line'), may hold values from 0.5 to 2
- drag: float32 [32, 256], P('line'), may hold values from 0.2 to 1
- span_column: int32 [32], replicated, may hold values from 0 to 31, each once
- segment_step: int32 [128], replicated, may hold values from 0 to 1, as said below
- transfer: float32 [32, 2, 512, 256], P('line'), may hold values from -0.75 to 0.75
- span_stiff: float32 [32, 512, 512], P('line')
- mass: float32 [32, 512], P('line'), may hold values from 0.02 to 0.08
- disp0: float32 [32, 512], P('line'), may hold values from -3 to 3
- vel0: float32 [32, 512], P('line'), may hold values from -3 to 3
- acc0: float32 [32, 512], P('line'), may hold values from -3 to 3
Outputs:
- disp_out: float32 [32, 512], P('line')
- vel_out: float32 [32, 512], P('line')
Inputs may be any that keep to these rules, and one draw needn't show every extreme that they name: `span_column`: every span number appears exactly once. `segment_step`: exactly half of the 128 segments load each of the two steps.
All inputs are finite; a program needn't handle non-finite values.
Results may differ from a plain program's by a relative error of at most 0.0003.
Values may be sent and summed in bfloat16 or wider, within the bound.
A program may use at most 128 MiB of HBM per device.

v0:
```python
import math

import jax
import jax.numpy as jnp
from jax import lax
from jax.sharding import PartitionSpec as P

Q = 256
KF = 64
TS = 64


accel_scale = 4.0
velocity_scale = 4.0
half_step = 0.5


def shifted(array, axis, by):
    length = lax.axis_size(axis)
    pairs = [(i, i + by) for i in range(length) if 0 <= i + by < length]
    return lax.ppermute(array, axis, pairs)


def exact_dot(first, second):
    return jnp.dot(
        first, second, precision=lax.Precision.HIGHEST, preferred_element_type=jnp.float32
    )


def trig_table(sample_count, freq_count):
    sample_index = jnp.arange(sample_count, dtype=jnp.float32)[:, None]
    frequency = (jnp.arange(freq_count, dtype=jnp.float32)[None, :] + 0.25) * (math.pi / freq_count)
    phase_angle = sample_index * frequency
    return jnp.concatenate([jnp.cos(phase_angle), jnp.sin(phase_angle)], axis=1).astype(
        jnp.bfloat16
    )


def cho_apply(factor, values):
    return jax.scipy.linalg.cho_solve((factor, True), values)


def blocked_cholesky(matrix):
    order = matrix.shape[0]
    panel_width = min(128, order)
    factor = jnp.zeros_like(matrix)
    trailing = matrix
    for start_row in range(0, order, panel_width):
        end_row = start_row + panel_width
        corner = jnp.linalg.cholesky(trailing[start_row:end_row, start_row:end_row])
        factor = factor.at[start_row:end_row, start_row:end_row].set(corner)
        if end_row < order:
            below = trailing[end_row:, start_row:end_row]
            below_factor = jax.scipy.linalg.solve_triangular(corner, below.T, lower=True).T
            factor = factor.at[end_row:, start_row:end_row].set(below_factor)
            trailing = trailing.at[end_row:, end_row:].add(-exact_dot(below_factor, below_factor.T))
    return factor


def local(
    gust_coef,
    mean_wind,
    drag,
    span_column,
    segment_step,
    transfer,
    span_stiff,
    mass,
    disp0,
    vel0,
    acc0,
):
    line_count = lax.axis_size("line")
    time_count = lax.axis_size("tm")
    line_pos = lax.axis_index("line")
    time_pos = lax.axis_index("tm")
    span_count = span_column.shape[0]
    block_order = span_stiff.shape[-1]
    seg_count = segment_step.shape[0]
    trig_rows = trig_table(TS, KF)
    spectra = gust_coef.reshape(2 * KF, span_count * Q)
    wind_field = jnp.dot(trig_rows, spectra, preferred_element_type=jnp.float32).astype(
        jnp.bfloat16
    )
    wind_field = jnp.take(wind_field.reshape(TS, span_count, Q), span_column, axis=1)
    left_map = transfer[0, 0]
    right_map = transfer[0, 1]
    window_scale = 1.0 / (TS * (seg_count // 2))
    arrived = lax.all_to_all(wind_field, "line", split_axis=1, concat_axis=0, tiled=True)
    arrived = arrived.reshape(line_count, TS, Q)
    seg_index = jnp.arange(line_count, dtype=jnp.int32) * time_count + time_pos
    seg_flags = jnp.take(segment_step, seg_index)
    span_block = span_stiff[0]
    before = shifted(span_block, "line", 1)
    identity = jnp.eye(block_order, dtype=jnp.float32)
    diag_block = span_block + before + (accel_scale * mass[0])[:, None] * identity
    coupled = (line_pos < line_count - 1).astype(jnp.float32)
    upper_block = -span_block * coupled
    lower_block = -before
    stored = []
    stride = 1
    while stride < line_count:
        factor = blocked_cholesky(diag_block)
        solved = cho_apply(factor, jnp.concatenate([lower_block, upper_block], axis=1))
        from_lower = shifted(solved, "line", stride)
        from_upper = shifted(solved, "line", -stride)
        new_diag = (
            diag_block
            - exact_dot(lower_block, from_lower[:, block_order:])
            - exact_dot(upper_block, from_upper[:, :block_order])
        )
        new_lower = -exact_dot(lower_block, from_lower[:, :block_order])
        new_upper = -exact_dot(upper_block, from_upper[:, block_order:])
        stored.append((factor, lower_block, upper_block))
        diag_block, lower_block, upper_block = (new_diag, new_lower, new_upper)
        stride = stride * 2
    final_factor = blocked_cholesky(diag_block)
    displacement, velocity, accel_now = (disp0, vel0, acc0)
    for window in range(2):
        next_velocity = shifted(velocity, "line", -1)
        offset = mean_wind - (exact_dot(velocity, left_map) + exact_dot(next_velocity, right_map))
        relative = arrived.astype(jnp.float32) + offset[None]
        weight = (seg_flags == window).astype(jnp.float32)
        window_partial_value = jnp.sum(
            weight[:, None, None] * relative * jnp.abs(relative), axis=(0, 1)
        )[None]
        summed = lax.psum(window_partial_value, "tm")
        span_load = drag * summed * window_scale
        passed = exact_dot(span_load, right_map.T)
        from_left = shifted(passed, "line", 1)
        force = exact_dot(span_load, left_map.T) + from_left
        right_side = force + mass * (
            accel_scale * displacement + velocity_scale * velocity + accel_now
        )
        vector = right_side[0]
        reach_now = 1
        for solve_factor, lower_one, upper_one in stored:
            solve_solved = cho_apply(solve_factor, vector)
            from_below = shifted(solve_solved, "line", reach_now)
            from_above = shifted(solve_solved, "line", -reach_now)
            vector = vector - exact_dot(lower_one, from_below) - exact_dot(upper_one, from_above)
            reach_now = reach_now * 2
        new_disp = cho_apply(final_factor, vector)[None]
        new_accel = accel_scale * (new_disp - displacement) - velocity_scale * velocity - accel_now
        velocity = velocity + half_step * (accel_now + new_accel)
        displacement, accel_now = (new_disp, new_accel)
    return (displacement, velocity)


def solution(mesh):
    return jax.shard_map(
        local,
        mesh=mesh,
        in_specs=(
            P(("line", "tm"), None, None, None),
            P("line", None),
            P("line", None),
            P(),
            P(),
            P("line", None, None, None),
            P("line", None, None),
            P("line", None),
            P("line", None),
            P("line", None),
            P("line", None),
        ),
        out_specs=(P("line", None), P("line", None)),
        check_vma=False,
    )
```

profile of v0, /device:TPU:1, one launch (start us, length us, event | category | flops | bytes accessed | tf_op | source)
XLA Modules:
  0.0 1562.0 jit_solution(14610299977705007109)
XLA Ops:
  63.4 11.7 cholesky.374
  92.9 11.7 cholesky.385
  123.0 11.7 cholesky.396
  151.1 11.9 cholesky.407
  181.8 40.1 %custom-call.54 = f32[4,128,128]{1,2,0:T(8,128)S(1)} custom-call(f32[4,128,128]{2,1,0:T(8,128)} %copy-done.57), custom_call_target="InvertDiagBlocksLowerTriangular" | custom-call | tf_op jit(solution)/shard_map/jit(_cho_solve)/triangular_solve | solution.py:40
  252.0 13.6 collective-permute-done.14
  275.6 11.7 cholesky.418
  301.9 11.7 cholesky.429
  325.9 11.7 cholesky.440
  349.8 11.7 cholesky.451
  371.8 40.4 %custom-call.58 = f32[4,128,128]{1,2,0:T(8,128)} custom-call(f32[4,128,128]{2,1,0:T(8,128)S(1)} %get-tuple-element.835), custom_call_target="InvertDiagBlocksLowerTriangular" | custom-call | tf_op jit(solution)/shard_map/jit(_cho_solve)/triangular_solve | solution.py:40
  449.4 33.6 %collective-permute-done.16 = f32[512]{0:T(512)S(1)} collective-permute-done((f32[512]{0:T(512)S(1)}, f32[512]{0:T(512)S(1)}, u32[]{:S(2)}, u32[]{:S(2)}) %collective-permute-start.16) | collective-permute-done | bytes 2080 | tf_op jit(solution)/shard_map/ppermute | solution.py:21
  597.8 41.2 %custom-call.62 = f32[4,128,128]{1,2,0:T(8,128)} custom-call(f32[4,128,128]{2,1,0:T(8,128)} %get-tuple-element.836), custom_call_target="InvertDiagBlocksLowerTriangular" | custom-call | tf_op jit(solution)/shard_map/jit(_cho_solve)/triangular_solve | solution.py:40
  682.3 28.2 %collective-permute-done.18 = f32[512]{0:T(512)S(1)} collective-permute-done((f32[512]{0:T(512)S(1)}, f32[512]{0:T(512)S(1)}, u32[]{:S(2)}, u32[]{:S(2)}) %collective-permute-start.18) | collective-permute-done | bytes 2080 | tf_op jit(solution)/shard_map/ppermute | solution.py:21
  712.4 44.7 %collective-permute-done.17 = f32[512]{0:T(512)S(1)} collective-permute-done((f32[512]{0:T(512)S(1)}, f32[512]{0:T(512)S(1)}, u32[]{:S(2)}, u32[]{:S(2)}) %collective-permute-start.17) | collective-permute-done | bytes 2080 | tf_op jit(solution)/shard_map/ppermute | solution.py:21
  766.5 12.5 cholesky.506
  802.3 12.5 cholesky.517
  865.5 12.5 cholesky.539
  884.4 14.0 while.97
  898.4 41.1 %custom-call.66 = f32[4,128,128]{1,2,0:T(8,128)} custom-call(f32[4,128,128]{2,1,0:T(8,128)} %get-tuple-element.837), custom_call_target="InvertDiagBlocksLowerTriangular" | custom-call | tf_op jit(solution)/shard_map/jit(_cho_solve)/triangular_solve | solution.py:40
  983.4 31.7 %collective-permute-done.20 = f32[512]{0:T(512)S(1)} collective-permute-done((f32[512]{0:T(512)S(1)}, f32[512]{0:T(512)S(1)}, u32[]{:S(2)}, u32[]{:S(2)}) %collective-permute-start.20) | collective-permute-done | bytes 2080 | tf_op jit(solution)/shard_map/ppermute | solution.py:21
  1027.9 12.5 cholesky.550
  1063.7 12.5 cholesky.561
  1127.0 12.5 cholesky.583
  1146.0 14.1 while.98
  1160.2 41.1 %custom-call.70 = f32[4,128,128]{1,2,0:T(8,128)} custom-call(f32[4,128,128]{2,1,0:T(8,128)} %get-tuple-element.838), custom_call_target="InvertDiagBlocksLowerTriangular" | custom-call | tf_op jit(solution)/shard_map/jit(_cho_solve)/triangular_solve | solution.py:40
  1239.6 30.0 %collective-permute-done.22 = f32[512]{0:T(512)S(1)} collective-permute-done((f32[512]{0:T(512)S(1)}, f32[512]{0:T(512)S(1)}, u32[]{:S(2)}, u32[]{:S(2)}) %collective-permute-start.22) | collective-permute-done | bytes 2080 | tf_op jit(solution)/shard_map/ppermute | solution.py:21
  1277.9 12.5 cholesky.594
  1313.6 12.5 cholesky.605
  1376.8 12.5 cholesky.627
  1395.9 13.6 while.99
  1409.5 40.7 %custom-call.85 = f32[4,128,128]{1,2,0:T(8,128)} custom-call(f32[4,128,128]{2,1,0:T(8,128)} %get-tuple-element.850), custom_call_target="InvertDiagBlocksLowerTriangular" | custom-call | tf_op jit(solution)/shard_map/jit(_cho_solve)/triangular_solve | solution.py:40
  (879 shorter events, 955.1 us)
Async XLA Ops:
  3.2 56.3 %collective-permute-start = (f32[512,512]{0,1:T(8,128)}, f32[512,512]{0,1:T(8,128)S(1)}, u32[]{:S(2)}, u32[]{:S(2)}) collective-permute-start(f32[512,512]{0,1:T(8,128)} %bitcast), channel_id=1, source_target_pairs={{0,4},{4,8},{8,12},{12,16},{16,20},{20,24},{24,28},{28,32},{32,36}... | collective-permute-start | bytes 3145736 | tf_op jit(solution)/shard_map/ppermute | solution.py:21
  18.0 24.1 %all-to-all-start = ((bf16[64,32,256]{2,0,1:T(8,128)(2,1)}), bf16[64,32,256]{2,0,1:T(8,128)(2,1)}, u32[]{:S(2)}, u32[]{:S(2)}) async-start(bf16[64,32,256]{2,0,1:T(8,128)(2,1)} %select_bitcast_fusion), calls=%async_computation | async-start | bytes 2097152 | tf_op jit(solution)/shard_map/all_to_all | solution.py:89
  25.1 9.4 collective-permute-start.11
  237.5 30.0 %collective-permute-start.2 = (f32[512,1024]{1,0:T(8,128)}, f32[512,1024]{1,0:T(8,128)}, u32[]{:S(2)}, u32[]{:S(2)}) collective-permute-start(f32[512,1024]{1,0:T(8,128)} %pad_maximum_fusion), channel_id=1, source_target_pairs={{4,0},{8,4},{12,8},{16,12},{20,16},{24,20},{28,24},{32,28},{36,32}... | collective-permute-start | bytes 6291464 | tf_op jit(solution)/shard_map/ppermute | solution.py:21
  239.4 31.1 %collective-permute-start.1 = (f32[512,1024]{1,0:T(8,128)}, f32[512,1024]{1,0:T(8,128)}, u32[]{:S(2)}, u32[]{:S(2)}) collective-permute-start(f32[512,1024]{1,0:T(8,128)} %pad_maximum_fusion), channel_id=1, source_target_pairs={{0,4},{4,8},{8,12},{12,16},{16,20},{20,24},{24,28},{28,32},{32,36}... | collective-permute-start | bytes 6291464 | tf_op jit(solution)/shard_map/ppermute | solution.py:21
  246.4 19.1 %collective-permute-start.14 = (f32[512]{0:T(512)S(1)}, f32[512]{0:T(512)S(1)}, u32[]{:S(2)}, u32[]{:S(2)}) collective-permute-start(f32[512]{0:T(512)S(1)} %bitcast.1958), channel_id=1, source_target_pairs={{4,0},{8,4},{12,8},{16,12},{20,16},{24,20},{28,24},{32,28},{36,32}... | collective-permute-start | bytes 6152 | tf_op jit(solution)/shard_map/ppermute | solution.py:21
  248.4 18.4 %collective-permute-start.13 = (f32[512]{0:T(512)S(1)}, f32[512]{0:T(512)S(1)}, u32[]{:S(2)}, u32[]{:S(2)}) collective-permute-start(f32[512]{0:T(512)S(1)} %bitcast.1959), channel_id=1, source_target_pairs={{0,4},{4,8},{8,12},{12,16},{16,20},{20,24},{24,28},{28,32},{32,36}... | collective-permute-start | bytes 6152 | tf_op jit(solution)/shard_map/ppermute | solution.py:21
  434.5 50.0 %collective-permute-start.4 = (f32[512,1024]{1,0:T(8,128)}, f32[512,1024]{1,0:T(8,128)}, u32[]{:S(2)}, u32[]{:S(2)}) collective-permute-start(f32[512,1024]{1,0:T(8,128)} %pad_maximum_fusion.1), channel_id=1, source_target_pairs={{8,0},{12,4},{16,8},{20,12},{24,16},{28,20},{32,24},{36,28},{40,32... | collective-permute-start | bytes 6291464 | tf_op jit(solution)/shard_map/ppermute | solution.py:21
  435.8 51.8 %collective-permute-start.3 = (f32[512,1024]{1,0:T(8,128)}, f32[512,1024]{1,0:T(8,128)}, u32[]{:S(2)}, u32[]{:S(2)}) collective-permute-start(f32[512,1024]{1,0:T(8,128)} %pad_maximum_fusion.1), channel_id=1, source_target_pairs={{0,8},{4,12},{8,16},{12,20},{16,24},{20,28},{24,32},{28,36},{32,40... | collective-permute-start | bytes 6291464 | tf_op jit(solution)/shard_map/ppermute | solution.py:21
  444.1 38.9 %collective-permute-start.16 = (f32[512]{0:T(512)S(1)}, f32[512]{0:T(512)S(1)}, u32[]{:S(2)}, u32[]{:S(2)}) collective-permute-start(f32[512]{0:T(512)S(1)} %bitcast.1960), channel_id=1, source_target_pairs={{8,0},{12,4},{16,8},{20,12},{24,16},{28,20},{32,24},{36,28},{40,32... | collective-permute-start | bytes 6152 | tf_op jit(solution)/shard_map/ppermute | solution.py:21
  445.4 38.5 %collective-permute-start.15 = (f32[512]{0:T(512)S(1)}, f32[512]{0:T(512)S(1)}, u32[]{:S(2)}, u32[]{:S(2)}) collective-permute-start(f32[512]{0:T(512)S(1)} %bitcast.1961), channel_id=1, source_target_pairs={{0,8},{4,12},{8,16},{12,20},{16,24},{20,28},{24,32},{28,36},{32,40... | collective-permute-start | bytes 6152 | tf_op jit(solution)/shard_map/ppermute | solution.py:21
  661.4 96.3 %collective-permute-start.6 = (f32[512,1024]{1,0:T(8,128)}, f32[512,1024]{1,0:T(8,128)}, u32[]{:S(2)}, u32[]{:S(2)}) collective-permute-start(f32[512,1024]{1,0:T(8,128)} %pad_maximum_fusion.2), channel_id=1, source_target_pairs={{16,0},{20,4},{24,8},{28,12},{32,16},{36,20},{40,24},{44,28},{48,3... | collective-permute-start | bytes 6291464 | tf_op jit(solution)/shard_map/ppermute | solution.py:21
  662.7 98.1 %collective-permute-start.5 = (f32[512,1024]{1,0:T(8,128)}, f32[512,1024]{1,0:T(8,128)}, u32[]{:S(2)}, u32[]{:S(2)}) collective-permute-start(f32[512,1024]{1,0:T(8,128)} %pad_maximum_fusion.2), channel_id=1, source_target_pairs={{0,16},{4,20},{8,24},{12,28},{16,32},{20,36},{24,40},{28,44},{32,4... | collective-permute-start | bytes 6291464 | tf_op jit(solution)/shard_map/ppermute | solution.py:21
  672.8 37.7 %collective-permute-start.18 = (f32[512]{0:T(512)S(1)}, f32[512]{0:T(512)S(1)}, u32[]{:S(2)}, u32[]{:S(2)}) collective-permute-start(f32[512]{0:T(512)S(1)} %bitcast.1962), channel_id=1, source_target_pairs={{16,0},{20,4},{24,8},{28,12},{32,16},{36,20},{40,24},{44,28},{48,3... | collective-permute-start | bytes 6152 | tf_op jit(solution)/shard_map/ppermute | solution.py:21
  674.1 82.9 %collective-permute-start.17 = (f32[512]{0:T(512)S(1)}, f32[512]{0:T(512)S(1)}, u32[]{:S(2)}, u32[]{:S(2)}) collective-permute-start(f32[512]{0:T(512)S(1)} %bitcast.1963), channel_id=1, source_target_pairs={{0,16},{4,20},{8,24},{12,28},{16,32},{20,36},{24,40},{28,44},{32,4... | collective-permute-start | bytes 6152 | tf_op jit(solution)/shard_map/ppermute | solution.py:21
  962.4 56.7 %collective-permute-start.8 = (f32[512,1024]{1,0:T(8,128)}, f32[512,1024]{1,0:T(8,128)}, u32[]{:S(2)}, u32[]{:S(2)}) collective-permute-start(f32[512,1024]{1,0:T(8,128)} %pad_maximum_fusion.3), channel_id=1, source_target_pairs={{32,0},{36,4},{40,8},{44,12},{48,16},{52,20},{56,24},{60,28},{64,3... | collective-permute-start | bytes 6291464 | tf_op jit(solution)/shard_map/ppermute | solution.py:21
  963.6 58.5 %collective-permute-start.7 = (f32[512,1024]{1,0:T(8,128)}, f32[512,1024]{1,0:T(8,128)}, u32[]{:S(2)}, u32[]{:S(2)}) collective-permute-start(f32[512,1024]{1,0:T(8,128)} %pad_maximum_fusion.3), channel_id=1, source_target_pairs={{0,32},{4,36},{8,40},{12,44},{16,48},{20,52},{24,56},{28,60},{32,6... | collective-permute-start | bytes 6291464 | tf_op jit(solution)/shard_map/ppermute | solution.py:21
  978.0 37.1 %collective-permute-start.20 = (f32[512]{0:T(512)S(1)}, f32[512]{0:T(512)S(1)}, u32[]{:S(2)}, u32[]{:S(2)}) collective-permute-start(f32[512]{0:T(512)S(1)} %bitcast.1964), channel_id=1, source_target_pairs={{32,0},{36,4},{40,8},{44,12},{48,16},{52,20},{56,24},{60,28},{64,3... | collective-permute-start | bytes 6152 | tf_op jit(solution)/shard_map/ppermute | solution.py:21
  979.3 37.7 %collective-permute-start.19 = (f32[512]{0:T(512)S(1)}, f32[512]{0:T(512)S(1)}, u32[]{:S(2)}, u32[]{:S(2)}) collective-permute-start(f32[512]{0:T(512)S(1)} %bitcast.1965), channel_id=1, source_target_pairs={{0,32},{4,36},{8,40},{12,44},{16,48},{20,52},{24,56},{28,60},{32,6... | collective-permute-start | bytes 6152 | tf_op jit(solution)/shard_map/ppermute | solution.py:21
  1222.8 48.6 %collective-permute-start.10 = (f32[512,1024]{1,0:T(8,128)S(1)}, f32[512,1024]{1,0:T(8,128)S(1)}, u32[]{:S(2)}, u32[]{:S(2)}) collective-permute-start(f32[512,1024]{1,0:T(8,128)S(1)} %pad_maximum_fusion.4), channel_id=1, source_target_pairs={{64,0},{68,4},{72,8},{76,12},{80,16},{84,20},{88,24},{92,28},{96,3... | collective-permute-start | bytes 6291464 | tf_op jit(solution)/shard_map/ppermute | solution.py:21
  1224.1 49.2 %collective-permute-start.9 = (f32[512,1024]{1,0:T(8,128)S(1)}, f32[512,1024]{1,0:T(8,128)S(1)}, u32[]{:S(2)}, u32[]{:S(2)}) collective-permute-start(f32[512,1024]{1,0:T(8,128)S(1)} %pad_maximum_fusion.4), channel_id=1, source_target_pairs={{0,64},{4,68},{8,72},{12,76},{16,80},{20,84},{24,88},{28,92},{32,9... | collective-permute-start | bytes 6291464 | tf_op jit(solution)/shard_map/ppermute | solution.py:21
  1232.8 36.9 %collective-permute-start.22 = (f32[512]{0:T(512)S(1)}, f32[512]{0:T(512)S(1)}, u32[]{:S(2)}, u32[]{:S(2)}) collective-permute-start(f32[512]{0:T(512)S(1)} %bitcast.1976), channel_id=1, source_target_pairs={{64,0},{68,4},{72,8},{76,12},{80,16},{84,20},{88,24},{92,28},{96,3... | collective-permute-start | bytes 6152 | tf_op jit(solution)/shard_map/ppermute | solution.py:21
  1234.1 36.6 %collective-permute-start.21 = (f32[512]{0:T(512)S(1)}, f32[512]{0:T(512)S(1)}, u32[]{:S(2)}, u32[]{:S(2)}) collective-permute-start(f32[512]{0:T(512)S(1)} %bitcast.1977), channel_id=1, source_target_pairs={{0,64},{4,68},{8,72},{12,76},{16,80},{20,84},{24,88},{28,92},{32,9... | collective-permute-start | bytes 6152 | tf_op jit(solution)/shard_map/ppermute | solution.py:21
  1465.4 8.1 collective-permute-start.23
  1496.7 7.5 collective-permute-start.26
  1508.6 7.5 collective-permute-start.28
  1509.9 6.9 collective-permute-start.27
  1520.4 8.6 collective-permute-start.30
  1521.7 8.0 collective-permute-start.29
  1533.4 11.8 collective-permute-start.32
  1534.7 11.2 collective-permute-start.31
  1549.5 6.8 collective-permute-start.34
  (75 other events, 1673.6 us)
where the time goes:
time: 1580 us; the launch traced here: 1560 us
  other arithmetic  807 us (51%)
  matrix products  244 us (15%)
  waiting for transfers between devices  197 us (12%)
  local copies, waits for them, and re-layouts  151 us (10%)
  starting transfers between devices  143 us (9%)
  blocking collectives  16 us (1%)
    another operation x72, other arithmetic, blocked_cholesky(): corner = jnp.linalg.cholesky(trailing[start_row:end_row, start_row:end_row])  305 us
    another operation x29, other arithmetic, cho_apply(): return jax.scipy.linalg.cho_solve((factor, True), values)  263 us
    another operation x36, other arithmetic, blocked_cholesky(): jax.scipy.linalg.solve_triangular(corner, below.T, lower=True)  205 us
    ppermute x35, waiting for transfers between devices, shifted(): return lax.ppermute(array, axis, pairs)  189 us
    ppermute x35, starting transfers between devices, shifted(): return lax.ppermute(array, axis, pairs)  136 us
    another operation x238, matrix products, cho_apply(): return jax.scipy.linalg.cho_solve((factor, True), values)  118 us
    dot_general x64, matrix products, exact_dot(): jnp.dot(first, second, precision=lax.Precision.HIGHEST, preferred_element...  107 us
    another operation x79, local copies, waits for them, and re-layouts, cho_apply(): return jax.scipy.linalg.cho_solve((factor, True), values)  75.6 us
  transfers between devices with their start and end apart: 36, of which 13 were waited for; matrix products, arithmetic and copies ran while one was open for 4% of the time, Pallas kernels for 0%

commit v1 on v0

--- a/solution.py
+++ b/solution.py
@@ -3,6 +3,8 @@
 import jax
 import jax.numpy as jnp
 from jax import lax
+from jax.experimental import pallas as pl
+from jax.experimental.pallas import tpu as pltpu
 from jax.sharding import PartitionSpec as P
 
 Q = 256
@@ -36,25 +38,63 @@
     )
 
 
-def cho_apply(factor, values):
-    return jax.scipy.linalg.cho_solve((factor, True), values)
-
-
-def blocked_cholesky(matrix):
-    order = matrix.shape[0]
-    panel_width = min(128, order)
-    factor = jnp.zeros_like(matrix)
-    trailing = matrix
-    for start_row in range(0, order, panel_width):
-        end_row = start_row + panel_width
-        corner = jnp.linalg.cholesky(trailing[start_row:end_row, start_row:end_row])
-        factor = factor.at[start_row:end_row, start_row:end_row].set(corner)
-        if end_row < order:
-            below = trailing[end_row:, start_row:end_row]
-            below_factor = jax.scipy.linalg.solve_triangular(corner, below.T, lower=True).T
-            factor = factor.at[end_row:, start_row:end_row].set(below_factor)
-            trailing = trailing.at[end_row:, end_row:].add(-exact_dot(below_factor, below_factor.T))
-    return factor
+def split_dot(first, second):
+    first_hi = first.astype(jnp.bfloat16)
+    first_lo = (first - first_hi.astype(jnp.float32)).astype(jnp.bfloat16)
+    second_hi = second.astype(jnp.bfloat16)
+    second_lo = (second - second_hi.astype(jnp.float32)).astype(jnp.bfloat16)
+    left = jnp.concatenate([first_hi, first_hi, first_lo], axis=1)
+    right = jnp.concatenate([second_hi, second_lo, second_hi], axis=0)
+    return jnp.dot(left, right, preferred_element_type=jnp.float32)
+
+
+def solve_kernel(diag_ref, sides_ref, inverse_ref, solved_ref):
+    order = diag_ref.shape[0]
+    rows = lax.broadcasted_iota(jnp.int32, (order, order), 0)
+    columns = lax.broadcasted_iota(jnp.int32, (order, order), 1)
+    on_diag = rows == columns
+    diag = diag_ref[...]
+    diag_row = jnp.sum(jnp.where(on_diag, diag, 0.0), axis=0, keepdims=True)
+    diag_col = jnp.sum(jnp.where(on_diag, diag, 0.0), axis=1, keepdims=True)
+    bound = jnp.max(jnp.sum(jnp.abs(diag), axis=1, keepdims=True) / diag_col)
+    scale = jnp.minimum(1.0, 1.8 / bound)
+    start = jnp.where(on_diag, 1.0, 0.0) * 2.0 - diag * (scale / diag_row)
+    inverse_ref[...] = (scale / diag_col) * start
+
+    def unfinished(state):
+        step, error = state
+        return (step < 60) & (error > 9e-6)
+
+    def iterate(state):
+        step, _ = state
+        current = inverse_ref[...]
+        residual = jnp.where(on_diag, 1.0, 0.0) - split_dot(diag_ref[...], current)
+        inverse_ref[...] = current + jnp.dot(
+            current.astype(jnp.bfloat16),
+            residual.astype(jnp.bfloat16),
+            preferred_element_type=jnp.float32,
+        )
+        return step + 1, jnp.sum(residual * residual)
+
+    lax.while_loop(unfinished, iterate, (jnp.int32(0), jnp.float32(1.0)))
+    solved_ref[...] = split_dot(inverse_ref[...], sides_ref[...])
+
+
+def solve_block(diag, sides):
+    order = diag.shape[0]
+    return pl.pallas_call(
+        solve_kernel,
+        out_shape=(
+            jax.ShapeDtypeStruct(diag.shape, jnp.float32),
+            jax.ShapeDtypeStruct(sides.shape, jnp.float32),
+        ),
+        in_specs=[pl.BlockSpec(memory_space=pltpu.VMEM)] * 2,
+        out_specs=[pl.BlockSpec(memory_space=pltpu.VMEM)] * 2,
+        compiler_params=pltpu.CompilerParams(vmem_limit_bytes=48 * 2**20),
+        cost_estimate=pl.CostEstimate(
+            flops=24 * order**3, bytes_accessed=24 * order**2, transcendentals=0
+        ),
+    )(diag, sides)
 
 
 def local(
@@ -100,8 +140,7 @@
     stored = []
     stride = 1
     while stride < line_count:
-        factor = blocked_cholesky(diag_block)
-        solved = cho_apply(factor, jnp.concatenate([lower_block, upper_block], axis=1))
+        inverse, solved = solve_block(diag_block, jnp.concatenate([lower_block, upper_block], axis=1))
         from_lower = shifted(solved, "line", stride)
         from_upper = shifted(solved, "line", -stride)
         new_diag = (
@@ -111,10 +150,10 @@
         )
         new_lower = -exact_dot(lower_block, from_lower[:, :block_order])
         new_upper = -exact_dot(upper_block, from_upper[:, block_order:])
-        stored.append((factor, lower_block, upper_block))
+        stored.append((inverse, lower_block, upper_block))
         diag_block, lower_block, upper_block = (new_diag, new_lower, new_upper)
         stride = stride * 2
-    final_factor = blocked_cholesky(diag_block)
+    final_inverse, _ = solve_block(diag_block, lower_block)
     displacement, velocity, accel_now = (disp0, vel0, acc0)
     for window in range(2):
         next_velocity = shifted(velocity, "line", -1)
@@ -134,13 +173,13 @@
         )
         vector = right_side[0]
         reach_now = 1
-        for solve_factor, lower_one, upper_one in stored:
-            solve_solved = cho_apply(solve_factor, vector)
+        for solve_inverse, lower_one, upper_one in stored:
+            solve_solved = exact_dot(solve_inverse, vector)
             from_below = shifted(solve_solved, "line", reach_now)
             from_above = shifted(solve_solved, "line", -reach_now)
             vector = vector - exact_dot(lower_one, from_below) - exact_dot(upper_one, from_above)
             reach_now = reach_now * 2
-        new_disp = cho_apply(final_factor, vector)[None]
+        new_disp = exact_dot(final_inverse, vector)[None]
         new_accel = accel_scale * (new_disp - displacement) - velocity_scale * velocity - accel_now
         velocity = velocity + half_step * (accel_now + new_accel)
         displacement, accel_now = (new_disp, new_accel)

time: 1580 us -> 530 us (0.34)
  other arithmetic: 807 us -> 17.7 us
  matrix products: 244 us -> 85.8 us
  local copies, waits for them, and re-layouts: 151 us -> 7.99 us
  Pallas kernels: 0 us -> 42.9 us
    another operation x138 -> x1, other arithmetic: 774 us -> 0.15 us  [the longest x72 305 us: blocked_cholesky(): corner = jnp.linalg.cholesky(trailing[start_row:end_row, start_row:end_row])]
    another operation x256 -> x0, matrix products: 137 us -> none  [the longest x238 118 us: cho_apply(): return jax.scipy.linalg.cho_solve((factor, True), values)]
    another operation x97 -> x0, local copies, waits for them, and re-layouts: 87.4 us -> none  [the longest x79 75.6 us: cho_apply(): return jax.scipy.linalg.cho_solve((factor, True), values)]
    pallas_call x0 -> x6, Pallas kernels: none -> 42.9 us  [solve_block(): pl.pallas_call(solve_kernel, out_shape=(jax.ShapeDtypeStruct(diag.shape,...]
    scatter x24 -> x0, local copies, waits for them, and re-layouts: 26.5 us -> none  [the longest x18 20 us: blocked_cholesky(): factor = factor.at[end_row:, start_row:end_row].set(below_factor)]
    dot_general x64 -> x59, matrix products: 107 us -> 85.3 us  [exact_dot(): jnp.dot(first, second, precision=lax.Precision.HIGHEST, preferred_element...]
    div x24 -> x0, other arithmetic: 16.8 us -> none  [blocked_cholesky(): corner = jnp.linalg.cholesky(trailing[start_row:end_row, start_row:end_row])]
    unnamed x144 -> x101, local copies, waits for them, and re-layouts: 19.4 us -> 3.36 us
  transfers between devices with their start and end apart: 36 -> 36, of which waited for: 13 -> 9; matrix products, arithmetic and copies ran while one was open for 4% -> 13% of each run, Pallas kernels for 0% -> 3%
where the time goes in v1:
time: 530 us; the launch traced here: 519 us
  waiting for transfers between devices  192 us (36%)
  starting transfers between devices  150 us (28%)
  matrix products  85.8 us (16%)
  Pallas kernels  42.9 us (8%)
  blocking collectives  20.3 us (4%)
  other arithmetic  17.7 us (3%)
  local copies, waits for them, and re-layouts  7.99 us (2%)
    ppermute x35, waiting for transfers between devices, shifted(): return lax.ppermute(array, axis, pairs)  192 us
    ppermute x35, starting transfers between devices, shifted(): return lax.ppermute(array, axis, pairs)  141 us
    dot_general x59, matrix products, exact_dot(): jnp.dot(first, second, precision=lax.Precision.HIGHEST, preferred_element...  85.3 us
    pallas_call x6, Pallas kernels, solve_block(): pl.pallas_call(solve_kernel, out_shape=(jax.ShapeDtypeStruct(diag.shape,...  42.9 us
    psum x2, blocking collectives, local(): summed = lax.psum(window_partial_value, 'tm')  20.3 us
  transfers between devices with their start and end apart: 36, of which 9 were waited for; matrix products, arithmetic and copies ran while one was open for 13% of the time, Pallas kernels for 3%

profile of v1, /device:TPU:1, one launch (start us, length us, event | category | flops | bytes accessed | tf_op | source)
XLA Modules:
  0.0 519.4 jit_solution(12400854340525373023)
XLA Ops:
  0.6 4.6 collective-permute-start
  5.9 11.3 %collective-permute-done = f32[512,512]{1,0:T(8,128)S(1)} collective-permute-done((f32[512,512]{1,0:T(8,128)}, f32[512,512]{1,0:T(8,128)S(1)}, u32[]{:S(2)}, u32[]{:S(2)}) %collective-permute-start) | collective-permute-done | bytes 1048608 | tf_op jit(solution)/shard_map/ppermute | solution.py:23
  21.1 8.0 %shard_map.122 = (f32[512,512]{1,0:T(8,128)S(1)}, f32[512,1024]{1,0:T(8,128)S(1)}) custom-call(f32[512,512]{1,0:T(8,128)S(1)} %get-tuple-element.29.diag_ref, f32[512,1024]{1,0:T(8,128)} %pad_maximum_fusion.sides_ref), custom_call_target="tpu_custom_call" | custom-call | flops 3221225472 | bytes 6291456 | tf_op jit(solution)/shard_map/pallas_call | solution.py:85
  31.2 4.5 collective-permute-start.1
  35.6 21.6 %collective-permute-done.2 = f32[512,1024]{1,0:T(8,128)S(1)} collective-permute-done((f32[512,1024]{1,0:T(8,128)S(1)}, f32[512,1024]{1,0:T(8,128)S(1)}, u32[]{:S(2)}, u32[]{:S(2)}) %collective-permute-start.2) | collective-permute-done | bytes 2097184 | tf_op jit(solution)/shard_map/ppermute | solution.py:23
  66.5 8.1 %shard_map.123 = (f32[512,512]{1,0:T(8,128)S(1)}, f32[512,1024]{1,0:T(8,128)}) custom-call(f32[512,512]{1,0:T(8,128)S(1)} %fusion.13.diag_ref, f32[512,1024]{1,0:T(8,128)} %pad_maximum_fusion.1.sides_ref), custom_call_target="tpu_custom_call" | custom-call | flops 3221225472 | bytes 6291456 | tf_op jit(solution)/shard_map/pallas_call | solution.py:85
  75.9 5.5 %collective-permute-start.3 = (f32[512,1024]{1,0:T(8,128)}, f32[512,1024]{1,0:T(8,128)}, u32[]{:S(2)}, u32[]{:S(2)}) collective-permute-start(f32[512,1024]{1,0:T(8,128)} %get-tuple-element.14), channel_id=1, source_target_pairs={{0,8},{4,12},{8,16},{12,20},{16,24},{20,28},{24,32},{28,36},{32,40... | collective-permute-start | bytes 6291464 | tf_op jit(solution)/shard_map/ppermute | solution.py:23
  89.8 9.7 %all-to-all-start = ((bf16[64,32,256]{2,0,1:T(8,128)(2,1)}), bf16[64,32,256]{2,0,1:T(8,128)(2,1)}, u32[]{:S(2)}, u32[]{:S(2)}) async-start(bf16[64,32,256]{2,0,1:T(8,128)(2,1)} %select_bitcast_fusion), calls=%async_computation | async-start | bytes 2097152 | tf_op jit(solution)/shard_map/all_to_all | solution.py:129
  102.9 29.7 %collective-permute-done.4 = f32[512,1024]{1,0:T(8,128)} collective-permute-done((f32[512,1024]{1,0:T(8,128)}, f32[512,1024]{1,0:T(8,128)}, u32[]{:S(2)}, u32[]{:S(2)}) %collective-permute-start.4) | collective-permute-done | bytes 2097184 | tf_op jit(solution)/shard_map/ppermute | solution.py:23
  147.9 8.1 %shard_map.124 = (f32[512,512]{1,0:T(8,128)S(1)}, f32[512,1024]{1,0:T(8,128)}) custom-call(f32[512,512]{1,0:T(8,128)S(1)} %fusion.11.diag_ref, f32[512,1024]{1,0:T(8,128)} %pad_maximum_fusion.2.sides_ref), custom_call_target="tpu_custom_call" | custom-call | flops 3221225472 | bytes 6291456 | tf_op jit(solution)/shard_map/pallas_call | solution.py:85
  157.7 6.9 %collective-permute-start.5 = (f32[512,1024]{1,0:T(8,128)}, f32[512,1024]{1,0:T(8,128)}, u32[]{:S(2)}, u32[]{:S(2)}) collective-permute-start(f32[512,1024]{1,0:T(8,128)} %get-tuple-element.15), channel_id=1, source_target_pairs={{0,16},{4,20},{8,24},{12,28},{16,32},{20,36},{24,40},{28,44},{32,4... | collective-permute-start | bytes 6291464 | tf_op jit(solution)/shard_map/ppermute | solution.py:23
  166.7 10.6 %psum.14 = f32[1,256]{1,0:T(1,128)S(1)} all-reduce(f32[1,256]{1,0:T(1,128)S(1)} %bitcast.318), channel_id=1, replica_groups=mesh['line'=32,'tm'=4] {'tm'}, use_global_device_ids=true, to_apply=%region_1.2 | all-reduce | flops 256 | bytes 2048 | tf_op jit(solution)/shard_map/psum | solution.py:166
  179.0 8.8 %collective-permute-start.12 = (f32[1,512]{1,0:T(1,128)S(1)}, f32[1,512]{1,0:T(1,128)S(1)}, u32[]{:S(2)}, u32[]{:S(2)}) collective-permute-start(f32[1,512]{1,0:T(1,128)S(1)} %fusion.44), channel_id=1, source_target_pairs={{0,4},{4,8},{8,12},{12,16},{16,20},{20,24},{24,28},{28,32},{32,36}... | collective-permute-start | bytes 6152 | tf_op jit(solution)/shard_map/ppermute | solution.py:23
  187.8 64.4 %collective-permute-done.12 = f32[1,512]{1,0:T(1,128)S(1)} collective-permute-done((f32[1,512]{1,0:T(1,128)S(1)}, f32[1,512]{1,0:T(1,128)S(1)}, u32[]{:S(2)}, u32[]{:S(2)}) %collective-permute-start.12) | collective-permute-done | bytes 2080 | tf_op jit(solution)/shard_map/ppermute | solution.py:23
  256.7 4.3 collective-permute-start.13
  276.5 6.8 %shard_map.125 = (f32[512,512]{1,0:T(8,128)S(1)}, f32[512,1024]{1,0:T(8,128)S(1)}) custom-call(f32[512,512]{1,0:T(8,128)S(1)} %fusion.10.diag_ref, f32[512,1024]{1,0:T(8,128)} %pad_maximum_fusion.3.sides_ref), custom_call_target="tpu_custom_call" | custom-call | flops 3221225472 | bytes 6291456 | tf_op jit(solution)/shard_map/pallas_call | solution.py:85
  286.3 4.1 collective-permute-start.7
  301.0 5.5 %collective-permute-start.17 = (f32[512]{0:T(512)S(1)}, f32[512]{0:T(512)S(1)}, u32[]{:S(2)}, u32[]{:S(2)}) collective-permute-start(f32[512]{0:T(512)S(1)} %bitcast.335), channel_id=1, source_target_pairs={{0,16},{4,20},{8,24},{12,28},{16,32},{20,36},{24,40},{28,44},{32,4... | collective-permute-start | bytes 6152 | tf_op jit(solution)/shard_map/ppermute | solution.py:23
  308.5 22.9 %collective-permute-done.8 = f32[512,1024]{1,0:T(8,128)S(1)} collective-permute-done((f32[512,1024]{1,0:T(8,128)S(1)}, f32[512,1024]{1,0:T(8,128)S(1)}, u32[]{:S(2)}, u32[]{:S(2)}) %collective-permute-start.8) | collective-permute-done | bytes 2097184 | tf_op jit(solution)/shard_map/ppermute | solution.py:23
  341.8 6.7 %shard_map.126 = (f32[512,512]{1,0:T(8,128)S(1)}, f32[512,1024]{1,0:T(8,128)S(1)}) custom-call(f32[512,512]{1,0:T(8,128)S(1)} %fusion.9.diag_ref, f32[512,1024]{1,0:T(8,128)} %pad_maximum_fusion.4.sides_ref), custom_call_target="tpu_custom_call" | custom-call | flops 3221225472 | bytes 6291456 | tf_op jit(solution)/shard_map/pallas_call | solution.py:85
  349.8 17.1 %collective-permute-start.9 = (f32[512,1024]{1,0:T(8,128)S(1)}, f32[512,1024]{1,0:T(8,128)S(1)}, u32[]{:S(2)}, u32[]{:S(2)}) collective-permute-start(f32[512,1024]{1,0:T(8,128)S(1)} %get-tuple-element.17), channel_id=1, source_target_pairs={{0,64},{4,68},{8,72},{12,76},{16,80},{20,84},{24,88},{28,92},{32,9... | collective-permute-start | bytes 6291464 | tf_op jit(solution)/shard_map/ppermute | solution.py:23
  369.2 4.7 collective-permute-start.19
  373.8 37.2 %collective-permute-done.20 = f32[512]{0:T(512)S(1)} collective-permute-done((f32[512]{0:T(512)S(1)}, f32[512]{0:T(512)S(1)}, u32[]{:S(2)}, u32[]{:S(2)}) %collective-permute-start.20) | collective-permute-done | bytes 2080 | tf_op jit(solution)/shard_map/ppermute | solution.py:23
  415.3 5.5 %collective-permute-start.21 = (f32[512]{0:T(512)S(1)}, f32[512]{0:T(512)S(1)}, u32[]{:S(2)}, u32[]{:S(2)}) collective-permute-start(f32[512]{0:T(512)S(1)} %bitcast.339), channel_id=1, source_target_pairs={{0,64},{4,68},{8,72},{12,76},{16,80},{20,84},{24,88},{28,92},{32,9... | collective-permute-start | bytes 6152 | tf_op jit(solution)/shard_map/ppermute | solution.py:23
  428.5 5.2 %shard_map.127 = (f32[512,512]{1,0:T(8,128)S(1)}, f32[512,512]{1,0:T(8,128)}) custom-call(f32[512,512]{1,0:T(8,128)S(1)} %fusion.8.diag_ref, f32[512,512]{1,0:T(8,128)S(1)} %convolution_negate_fusion.sides_ref), custom_call_target="tpu_custom_call" | custom-call | flops 3221225472 | bytes 6291456 | tf_op jit(solution)/shard_map/pallas_call | solution.py:85
  435.7 7.0 %collective-permute-start.23 = (f32[1,512]{1,0:T(1,128)S(1)}, f32[1,512]{1,0:T(1,128)S(1)}, u32[]{:S(2)}, u32[]{:S(2)}) collective-permute-start(f32[1,512]{1,0:T(1,128)S(1)} %get-tuple-element.26), channel_id=1, source_target_pairs={{4,0},{8,4},{12,8},{16,12},{20,16},{24,20},{28,24},{32,28},{36,32}... | collective-permute-start | bytes 6152 | tf_op jit(solution)/shard_map/ppermute | solution.py:23
  448.4 9.8 %psum.15 = f32[1,256]{1,0:T(1,128)S(1)} all-reduce(f32[1,256]{1,0:T(1,128)S(1)} %bitcast.317), channel_id=1, replica_groups=mesh['line'=32,'tm'=4] {'tm'}, use_global_device_ids=true, to_apply=%region_3.4 | all-reduce | flops 256 | bytes 2048 | tf_op jit(solution)/shard_map/psum | solution.py:166
  459.9 4.2 collective-permute-start.24
  469.1 4.2 collective-permute-start.25
  485.9 5.5 %collective-permute-start.29 = (f32[512]{0:T(512)S(1)}, f32[512]{0:T(512)S(1)}, u32[]{:S(2)}, u32[]{:S(2)}) collective-permute-start(f32[512]{0:T(512)S(1)} %bitcast.327), channel_id=1, source_target_pairs={{0,16},{4,20},{8,24},{12,28},{16,32},{20,36},{24,40},{28,44},{32,4... | collective-permute-start | bytes 6152 | tf_op jit(solution)/shard_map/ppermute | solution.py:23
  495.7 7.9 %collective-permute-start.31 = (f32[512]{0:T(512)S(1)}, f32[512]{0:T(512)S(1)}, u32[]{:S(2)}, u32[]{:S(2)}) collective-permute-start(f32[512]{0:T(512)S(1)} %bitcast.329), channel_id=1, source_target_pairs={{0,32},{4,36},{8,40},{12,44},{16,48},{20,52},{24,56},{28,60},{32,6... | collective-permute-start | bytes 6152 | tf_op jit(solution)/shard_map/ppermute | solution.py:23
  508.0 7.5 %collective-permute-start.33 = (f32[512]{0:T(512)S(1)}, f32[512]{0:T(512)S(1)}, u32[]{:S(2)}, u32[]{:S(2)}) collective-permute-start(f32[512]{0:T(512)S(1)} %bitcast.331), channel_id=1, source_target_pairs={{0,64},{4,68},{8,72},{12,76},{16,80},{20,84},{24,88},{28,92},{32,9... | collective-permute-start | bytes 6152 | tf_op jit(solution)/shard_map/ppermute | solution.py:23
  (248 shorter events, 149.4 us)
Async XLA Ops:
  0.6 16.6 %collective-permute-start = (f32[512,512]{1,0:T(8,128)}, f32[512,512]{1,0:T(8,128)S(1)}, u32[]{:S(2)}, u32[]{:S(2)}) collective-permute-start(f32[512,512]{1,0:T(8,128)} %bitcast.270), channel_id=1, source_target_pairs={{0,4},{4,8},{8,12},{12,16},{16,20},{20,24},{24,28},{28,32},{32,36}... | collective-permute-start | bytes 3145736 | tf_op jit(solution)/shard_map/ppermute | solution.py:23
  29.1 28.1 %collective-permute-start.2 = (f32[512,1024]{1,0:T(8,128)S(1)}, f32[512,1024]{1,0:T(8,128)S(1)}, u32[]{:S(2)}, u32[]{:S(2)}) collective-permute-start(f32[512,1024]{1,0:T(8,128)S(1)} %get-tuple-element.13), channel_id=1, source_target_pairs={{4,0},{8,4},{12,8},{16,12},{20,16},{24,20},{28,24},{32,28},{36,32}... | collective-permute-start | bytes 6291464 | tf_op jit(solution)/shard_map/ppermute | solution.py:23
  31.2 27.9 %collective-permute-start.1 = (f32[512,1024]{1,0:T(8,128)S(1)}, f32[512,1024]{1,0:T(8,128)S(1)}, u32[]{:S(2)}, u32[]{:S(2)}) collective-permute-start(f32[512,1024]{1,0:T(8,128)S(1)} %get-tuple-element.13), channel_id=1, source_target_pairs={{0,4},{4,8},{8,12},{12,16},{16,20},{20,24},{24,28},{28,32},{32,36}... | collective-permute-start | bytes 6291464 | tf_op jit(solution)/shard_map/ppermute | solution.py:23
  74.6 58.0 %collective-permute-start.4 = (f32[512,1024]{1,0:T(8,128)}, f32[512,1024]{1,0:T(8,128)}, u32[]{:S(2)}, u32[]{:S(2)}) collective-permute-start(f32[512,1024]{1,0:T(8,128)} %get-tuple-element.14), channel_id=1, source_target_pairs={{8,0},{12,4},{16,8},{20,12},{24,16},{28,20},{32,24},{36,28},{40,32... | collective-permute-start | bytes 6291464 | tf_op jit(solution)/shard_map/ppermute | solution.py:23
  75.9 60.1 %collective-permute-start.3 = (f32[512,1024]{1,0:T(8,128)}, f32[512,1024]{1,0:T(8,128)}, u32[]{:S(2)}, u32[]{:S(2)}) collective-permute-start(f32[512,1024]{1,0:T(8,128)} %get-tuple-element.14), channel_id=1, source_target_pairs={{0,8},{4,12},{8,16},{12,20},{16,24},{20,28},{24,32},{28,36},{32,40... | collective-permute-start | bytes 6291464 | tf_op jit(solution)/shard_map/ppermute | solution.py:23
  89.8 75.1 %all-to-all-start = ((bf16[64,32,256]{2,0,1:T(8,128)(2,1)}), bf16[64,32,256]{2,0,1:T(8,128)(2,1)}, u32[]{:S(2)}, u32[]{:S(2)}) async-start(bf16[64,32,256]{2,0,1:T(8,128)(2,1)} %select_bitcast_fusion), calls=%async_computation | async-start | bytes 2097152 | tf_op jit(solution)/shard_map/all_to_all | solution.py:129
  99.5 65.1 %collective-permute-start.11 = (f32[1,512]{1,0:T(1,128)S(1)}, f32[1,512]{1,0:T(1,128)S(1)}, u32[]{:S(2)}, u32[]{:S(2)}) collective-permute-start(f32[1,512]{1,0:T(1,128)S(1)} %copy-done.42), channel_id=1, source_target_pairs={{4,0},{8,4},{12,8},{16,12},{20,16},{24,20},{28,24},{32,28},{36,32}... | collective-permute-start | bytes 6152 | tf_op jit(solution)/shard_map/ppermute | solution.py:23
  156.0 106.1 %collective-permute-start.6 = (f32[512,1024]{1,0:T(8,128)}, f32[512,1024]{1,0:T(8,128)}, u32[]{:S(2)}, u32[]{:S(2)}) collective-permute-start(f32[512,1024]{1,0:T(8,128)} %get-tuple-element.15), channel_id=1, source_target_pairs={{16,0},{20,4},{24,8},{28,12},{32,16},{36,20},{40,24},{44,28},{48,3... | collective-permute-start | bytes 6291464 | tf_op jit(solution)/shard_map/ppermute | solution.py:23
  157.7 107.5 %collective-permute-start.5 = (f32[512,1024]{1,0:T(8,128)}, f32[512,1024]{1,0:T(8,128)}, u32[]{:S(2)}, u32[]{:S(2)}) collective-permute-start(f32[512,1024]{1,0:T(8,128)} %get-tuple-element.15), channel_id=1, source_target_pairs={{0,16},{4,20},{8,24},{12,28},{16,32},{20,36},{24,40},{28,44},{32,4... | collective-permute-start | bytes 6291464 | tf_op jit(solution)/shard_map/ppermute | solution.py:23
  179.0 73.2 %collective-permute-start.12 = (f32[1,512]{1,0:T(1,128)S(1)}, f32[1,512]{1,0:T(1,128)S(1)}, u32[]{:S(2)}, u32[]{:S(2)}) collective-permute-start(f32[1,512]{1,0:T(1,128)S(1)} %fusion.44), channel_id=1, source_target_pairs={{0,4},{4,8},{8,12},{12,16},{16,20},{20,24},{24,28},{28,32},{32,36}... | collective-permute-start | bytes 6152 | tf_op jit(solution)/shard_map/ppermute | solution.py:23
  254.7 6.3 %collective-permute-start.14 = (f32[512]{0:T(512)S(1)}, f32[512]{0:T(512)S(1)}, u32[]{:S(2)}, u32[]{:S(2)}) collective-permute-start(f32[512]{0:T(512)S(1)} %bitcast.319), channel_id=1, source_target_pairs={{4,0},{8,4},{12,8},{16,12},{20,16},{24,20},{28,24},{32,28},{36,32}... | collective-permute-start | bytes 6152 | tf_op jit(solution)/shard_map/ppermute | solution.py:23
  256.7 28.6 %collective-permute-start.13 = (f32[512]{0:T(512)S(1)}, f32[512]{0:T(512)S(1)}, u32[]{:S(2)}, u32[]{:S(2)}) collective-permute-start(f32[512]{0:T(512)S(1)} %bitcast.320), channel_id=1, source_target_pairs={{0,4},{4,8},{8,12},{12,16},{16,20},{20,24},{24,28},{28,32},{32,36}... | collective-permute-start | bytes 6152 | tf_op jit(solution)/shard_map/ppermute | solution.py:23
  283.4 48.1 %collective-permute-start.8 = (f32[512,1024]{1,0:T(8,128)S(1)}, f32[512,1024]{1,0:T(8,128)S(1)}, u32[]{:S(2)}, u32[]{:S(2)}) collective-permute-start(f32[512,1024]{1,0:T(8,128)S(1)} %get-tuple-element.16), channel_id=1, source_target_pairs={{32,0},{36,4},{40,8},{44,12},{48,16},{52,20},{56,24},{60,28},{64,3... | collective-permute-start | bytes 6291464 | tf_op jit(solution)/shard_map/ppermute | solution.py:23
  286.3 48.2 %collective-permute-start.7 = (f32[512,1024]{1,0:T(8,128)S(1)}, f32[512,1024]{1,0:T(8,128)S(1)}, u32[]{:S(2)}, u32[]{:S(2)}) collective-permute-start(f32[512,1024]{1,0:T(8,128)S(1)} %get-tuple-element.16), channel_id=1, source_target_pairs={{0,32},{4,36},{8,40},{12,44},{16,48},{20,52},{24,56},{28,60},{32,6... | collective-permute-start | bytes 6291464 | tf_op jit(solution)/shard_map/ppermute | solution.py:23
  291.4 5.3 %collective-permute-start.16 = (f32[512]{0:T(512)S(1)}, f32[512]{0:T(512)S(1)}, u32[]{:S(2)}, u32[]{:S(2)}) collective-permute-start(f32[512]{0:T(512)S(1)} %bitcast.332), channel_id=1, source_target_pairs={{8,0},{12,4},{16,8},{20,12},{24,16},{28,20},{32,24},{36,28},{40,32... | collective-permute-start | bytes 6152 | tf_op jit(solution)/shard_map/ppermute | solution.py:23
  299.7 6.8 %collective-permute-start.18 = (f32[512]{0:T(512)S(1)}, f32[512]{0:T(512)S(1)}, u32[]{:S(2)}, u32[]{:S(2)}) collective-permute-start(f32[512]{0:T(512)S(1)} %bitcast.334), channel_id=1, source_target_pairs={{16,0},{20,4},{24,8},{28,12},{32,16},{36,20},{40,24},{44,28},{48,3... | collective-permute-start | bytes 6152 | tf_op jit(solution)/shard_map/ppermute | solution.py:23
  301.0 6.5 %collective-permute-start.17 = (f32[512]{0:T(512)S(1)}, f32[512]{0:T(512)S(1)}, u32[]{:S(2)}, u32[]{:S(2)}) collective-permute-start(f32[512]{0:T(512)S(1)} %bitcast.335), channel_id=1, source_target_pairs={{0,16},{4,20},{8,24},{12,28},{16,32},{20,36},{24,40},{28,44},{32,4... | collective-permute-start | bytes 6152 | tf_op jit(solution)/shard_map/ppermute | solution.py:23
  348.4 74.4 %collective-permute-start.10 = (f32[512,1024]{1,0:T(8,128)S(1)}, f32[512,1024]{1,0:T(8,128)S(1)}, u32[]{:S(2)}, u32[]{:S(2)}) collective-permute-start(f32[512,1024]{1,0:T(8,128)S(1)} %get-tuple-element.17), channel_id=1, source_target_pairs={{64,0},{68,4},{72,8},{76,12},{80,16},{84,20},{88,24},{92,28},{96,3... | collective-permute-start | bytes 6291464 | tf_op jit(solution)/shard_map/ppermute | solution.py:23
  349.8 75.0 %collective-permute-start.9 = (f32[512,1024]{1,0:T(8,128)S(1)}, f32[512,1024]{1,0:T(8,128)S(1)}, u32[]{:S(2)}, u32[]{:S(2)}) collective-permute-start(f32[512,1024]{1,0:T(8,128)S(1)} %get-tuple-element.17), channel_id=1, source_target_pairs={{0,64},{4,68},{8,72},{12,76},{16,80},{20,84},{24,88},{28,92},{32,9... | collective-permute-start | bytes 6291464 | tf_op jit(solution)/shard_map/ppermute | solution.py:23
  367.9 43.2 %collective-permute-start.20 = (f32[512]{0:T(512)S(1)}, f32[512]{0:T(512)S(1)}, u32[]{:S(2)}, u32[]{:S(2)}) collective-permute-start(f32[512]{0:T(512)S(1)} %bitcast.336), channel_id=1, source_target_pairs={{32,0},{36,4},{40,8},{44,12},{48,16},{52,20},{56,24},{60,28},{64,3... | collective-permute-start | bytes 6152 | tf_op jit(solution)/shard_map/ppermute | solution.py:23
  369.2 42.8 %collective-permute-start.19 = (f32[512]{0:T(512)S(1)}, f32[512]{0:T(512)S(1)}, u32[]{:S(2)}, u32[]{:S(2)}) collective-permute-start(f32[512]{0:T(512)S(1)} %bitcast.337), channel_id=1, source_target_pairs={{0,32},{4,36},{8,40},{12,44},{16,48},{20,52},{24,56},{28,60},{32,6... | collective-permute-start | bytes 6152 | tf_op jit(solution)/shard_map/ppermute | solution.py:23
  414.0 6.8 %collective-permute-start.22 = (f32[512]{0:T(512)S(1)}, f32[512]{0:T(512)S(1)}, u32[]{:S(2)}, u32[]{:S(2)}) collective-permute-start(f32[512]{0:T(512)S(1)} %bitcast.338), channel_id=1, source_target_pairs={{64,0},{68,4},{72,8},{76,12},{80,16},{84,20},{88,24},{92,28},{96,3... | collective-permute-start | bytes 6152 | tf_op jit(solution)/shard_map/ppermute | solution.py:23
  415.3 6.5 %collective-permute-start.21 = (f32[512]{0:T(512)S(1)}, f32[512]{0:T(512)S(1)}, u32[]{:S(2)}, u32[]{:S(2)}) collective-permute-start(f32[512]{0:T(512)S(1)} %bitcast.339), channel_id=1, source_target_pairs={{0,64},{4,68},{8,72},{12,76},{16,80},{20,84},{24,88},{28,92},{32,9... | collective-permute-start | bytes 6152 | tf_op jit(solution)/shard_map/ppermute | solution.py:23
  435.7 10.7 %collective-permute-start.23 = (f32[1,512]{1,0:T(1,128)S(1)}, f32[1,512]{1,0:T(1,128)S(1)}, u32[]{:S(2)}, u32[]{:S(2)}) collective-permute-start(f32[1,512]{1,0:T(1,128)S(1)} %get-tuple-element.26), channel_id=1, source_target_pairs={{4,0},{8,4},{12,8},{16,12},{20,16},{24,20},{28,24},{32,28},{36,32}... | collective-permute-start | bytes 6152 | tf_op jit(solution)/shard_map/ppermute | solution.py:23
  467.2 6.1 %collective-permute-start.26 = (f32[512]{0:T(512)S(1)}, f32[512]{0:T(512)S(1)}, u32[]{:S(2)}, u32[]{:S(2)}) collective-permute-start(f32[512]{0:T(512)S(1)} %bitcast.322), channel_id=1, source_target_pairs={{4,0},{8,4},{12,8},{16,12},{20,16},{24,20},{28,24},{32,28},{36,32}... | collective-permute-start | bytes 6152 | tf_op jit(solution)/shard_map/ppermute | solution.py:23
  476.2 5.3 %collective-permute-start.28 = (f32[512]{0:T(512)S(1)}, f32[512]{0:T(512)S(1)}, u32[]{:S(2)}, u32[]{:S(2)}) collective-permute-start(f32[512]{0:T(512)S(1)} %bitcast.324), channel_id=1, source_target_pairs={{8,0},{12,4},{16,8},{20,12},{24,16},{28,20},{32,24},{36,28},{40,32... | collective-permute-start | bytes 6152 | tf_op jit(solution)/shard_map/ppermute | solution.py:23
  484.6 6.8 %collective-permute-start.30 = (f32[512]{0:T(512)S(1)}, f32[512]{0:T(512)S(1)}, u32[]{:S(2)}, u32[]{:S(2)}) collective-permute-start(f32[512]{0:T(512)S(1)} %bitcast.326), channel_id=1, source_target_pairs={{16,0},{20,4},{24,8},{28,12},{32,16},{36,20},{40,24},{44,28},{48,3... | collective-permute-start | bytes 6152 | tf_op jit(solution)/shard_map/ppermute | solution.py:23
  485.9 6.5 %collective-permute-start.29 = (f32[512]{0:T(512)S(1)}, f32[512]{0:T(512)S(1)}, u32[]{:S(2)}, u32[]{:S(2)}) collective-permute-start(f32[512]{0:T(512)S(1)} %bitcast.327), channel_id=1, source_target_pairs={{0,16},{4,20},{8,24},{12,28},{16,32},{20,36},{24,40},{28,44},{32,4... | collective-permute-start | bytes 6152 | tf_op jit(solution)/shard_map/ppermute | solution.py:23
  494.4 9.2 %collective-permute-start.32 = (f32[512]{0:T(512)S(1)}, f32[512]{0:T(512)S(1)}, u32[]{:S(2)}, u32[]{:S(2)}) collective-permute-start(f32[512]{0:T(512)S(1)} %bitcast.328), channel_id=1, source_target_pairs={{32,0},{36,4},{40,8},{44,12},{48,16},{52,20},{56,24},{60,28},{64,3... | collective-permute-start | bytes 6152 | tf_op jit(solution)/shard_map/ppermute | solution.py:23
  495.7 8.9 %collective-permute-start.31 = (f32[512]{0:T(512)S(1)}, f32[512]{0:T(512)S(1)}, u32[]{:S(2)}, u32[]{:S(2)}) collective-permute-start(f32[512]{0:T(512)S(1)} %bitcast.329), channel_id=1, source_target_pairs={{0,32},{4,36},{8,40},{12,44},{16,48},{20,52},{24,56},{28,60},{32,6... | collective-permute-start | bytes 6152 | tf_op jit(solution)/shard_map/ppermute | solution.py:23
  506.7 8.8 %collective-permute-start.34 = (f32[512]{0:T(512)S(1)}, f32[512]{0:T(512)S(1)}, u32[]{:S(2)}, u32[]{:S(2)}) collective-permute-start(f32[512]{0:T(512)S(1)} %bitcast.330), channel_id=1, source_target_pairs={{64,0},{68,4},{72,8},{76,12},{80,16},{84,20},{88,24},{92,28},{96,3... | collective-permute-start | bytes 6152 | tf_op jit(solution)/shard_map/ppermute | solution.py:23
  508.0 8.5 %collective-permute-start.33 = (f32[512]{0:T(512)S(1)}, f32[512]{0:T(512)S(1)}, u32[]{:S(2)}, u32[]{:S(2)}) collective-permute-start(f32[512]{0:T(512)S(1)} %bitcast.331), channel_id=1, source_target_pairs={{0,64},{4,68},{8,72},{12,76},{16,80},{20,84},{24,88},{28,92},{32,9... | collective-permute-start | bytes 6152 | tf_op jit(solution)/shard_map/ppermute | solution.py:23
  (54 other events, 1719.8 us)

commit v2 on v0

--- a/solution.py
+++ b/solution.py
@@ -3,6 +3,8 @@
 import jax
 import jax.numpy as jnp
 from jax import lax
+from jax.experimental import pallas as pl
+from jax.experimental.pallas import tpu as pltpu
 from jax.sharding import PartitionSpec as P
 
 Q = 256
@@ -57,39 +59,25 @@
     return factor
 
 
-def local(
-    gust_coef,
+def checked_loop(
+    line_count,
+    time_count,
+    arrived,
+    seg_flags,
     mean_wind,
     drag,
-    span_column,
-    segment_step,
     transfer,
     span_stiff,
     mass,
     disp0,
     vel0,
     acc0,
+    window_scale,
 ):
-    line_count = lax.axis_size("line")
-    time_count = lax.axis_size("tm")
     line_pos = lax.axis_index("line")
-    time_pos = lax.axis_index("tm")
-    span_count = span_column.shape[0]
     block_order = span_stiff.shape[-1]
-    seg_count = segment_step.shape[0]
-    trig_rows = trig_table(TS, KF)
-    spectra = gust_coef.reshape(2 * KF, span_count * Q)
-    wind_field = jnp.dot(trig_rows, spectra, preferred_element_type=jnp.float32).astype(
-        jnp.bfloat16
-    )
-    wind_field = jnp.take(wind_field.reshape(TS, span_count, Q), span_column, axis=1)
     left_map = transfer[0, 0]
     right_map = transfer[0, 1]
-    window_scale = 1.0 / (TS * (seg_count // 2))
-    arrived = lax.all_to_all(wind_field, "line", split_axis=1, concat_axis=0, tiled=True)
-    arrived = arrived.reshape(line_count, TS, Q)
-    seg_index = jnp.arange(line_count, dtype=jnp.int32) * time_count + time_pos
-    seg_flags = jnp.take(segment_step, seg_index)
     span_block = span_stiff[0]
     before = shifted(span_block, "line", 1)
     identity = jnp.eye(block_order, dtype=jnp.float32)
@@ -147,6 +135,736 @@
     return (displacement, velocity)
 
 
+MESH = pl.DeviceIdType.MESH
+
+
+def halves(value):
+    high = value.astype(jnp.bfloat16)
+    return high, (value - high.astype(jnp.float32)).astype(jnp.bfloat16)
+
+
+def split_dot(first, second, first_axis=1, second_axis=0):
+    first_hi, first_lo = halves(first)
+    second_hi, second_lo = halves(second)
+    left = jnp.concatenate([first_hi, first_hi, first_lo], axis=first_axis)
+    right = jnp.concatenate([second_hi, second_lo, second_hi], axis=second_axis)
+    return lax.dot_general(
+        left,
+        right,
+        (((first_axis,), (second_axis,)), ((), ())),
+        preferred_element_type=jnp.float32,
+    )
+
+
+def single_dot(first, second):
+    return jnp.dot(
+        first.astype(jnp.bfloat16), second.astype(jnp.bfloat16), preferred_element_type=jnp.float32
+    )
+
+
+def eye_mask(order):
+    rows = lax.broadcasted_iota(jnp.int32, (order, order), 0)
+    return rows == lax.broadcasted_iota(jnp.int32, (order, order), 1)
+
+
+LANES = 128
+
+
+def to_column(row):
+    mask = eye_mask(LANES)
+    parts = [
+        jnp.sum(jnp.where(mask, row[:, k : k + LANES], 0.0), axis=1, keepdims=True)
+        for k in range(0, row.shape[1], LANES)
+    ]
+    return jnp.concatenate(parts, axis=0)
+
+
+def to_row(column):
+    mask = eye_mask(LANES)
+    parts = [
+        jnp.sum(jnp.where(mask, column[k : k + LANES], 0.0), axis=0, keepdims=True)
+        for k in range(0, column.shape[0], LANES)
+    ]
+    return jnp.concatenate(parts, axis=1)
+
+
+def vec_mat(column, matrix):
+    return jnp.sum(column * matrix, axis=0, keepdims=True)
+
+
+def mat_vec(matrix, row):
+    return jnp.sum(matrix * row, axis=1, keepdims=True)
+
+
+def newton_inverse(diag_ref, inverse_ref, bad_ref, bound_on_residual=9e-6):
+    order = diag_ref.shape[0]
+    mask = eye_mask(order)
+    diag = diag_ref[...]
+    on_diag = jnp.where(mask, diag, 0.0)
+    diag_row = jnp.sum(on_diag, axis=0, keepdims=True)
+    diag_col = jnp.sum(on_diag, axis=1, keepdims=True)
+    bound = jnp.max(
+        jnp.sum(jnp.abs(diag), axis=0, keepdims=True) / diag_row, axis=1, keepdims=True
+    )
+    scale = jnp.minimum(1.0, 1.8 / bound)
+    identity = jnp.where(mask, 1.0, 0.0)
+    inverse_ref[...] = (scale / diag_col) * (2.0 * identity - diag * (scale / diag_row))
+    current = inverse_ref[...]
+    residual = identity - single_dot(diag_ref[...], current)
+    inverse_ref[...] = current + single_dot(current, residual)
+    for _ in range(2):
+        current = inverse_ref[...]
+        residual = identity - split_dot(diag_ref[...], current)
+        inverse_ref[...] = current + single_dot(current, residual)
+    size = jnp.sum(jnp.sum(residual * residual, axis=0, keepdims=True), axis=1, keepdims=True)
+    bad_ref[...] = bad_ref[...] + jnp.where(size < bound_on_residual, 0.0, 1.0)
+
+
+def line_kernel(
+    line_count,
+    time_count,
+    window_scale,
+    levels,
+    weight_ref,
+    wind_ref,
+    mean_ref,
+    drag_ref,
+    maps_ref,
+    span_ref,
+    mass_ref,
+    disp_in,
+    vel_in,
+    acc_in,
+    disp_ref,
+    vel_ref,
+    bad_out,
+    acc_ref,
+    bad_ref,
+    side_ref,
+    diag_ref,
+    inverse_ref,
+    prev_span,
+    prev_map,
+    next_vel,
+    couple,
+    update,
+    scaled,
+    update_out,
+    couple_out,
+    vec_out,
+    vec_in,
+    load_out,
+    load_in,
+    sol_out,
+    sol_in,
+    span_sems,
+    map_sems,
+    vel_sems,
+    update_sems,
+    couple_sems,
+    vec_sems,
+    load_send_sems,
+    load_recv_sems,
+    sol_sems,
+):
+    line = lax.axis_index("line")
+    time = lax.axis_index("tm")
+    core = lax.rem(line, 2)
+    order = span_ref.shape[1]
+    last = line_count - 1
+
+    barrier = pltpu.get_barrier_semaphore()
+    partners = jnp.int32(0)
+    for delta in (-1, 1):
+        there = (line + delta >= 0) & (line + delta <= last)
+        for turn in range(time_count):
+
+            @pl.when(there)
+            def _():
+                pl.semaphore_signal(
+                    barrier,
+                    inc=1,
+                    device_id=(line + delta, lax.rem(time + turn, time_count)),
+                    device_id_type=MESH,
+                )
+
+        partners = partners + jnp.where(there, time_count, 0)
+    for turn in range(1, time_count):
+        pl.semaphore_signal(
+            barrier,
+            inc=1,
+            device_id=(line, lax.rem(time + turn, time_count)),
+            device_id_type=MESH,
+        )
+    partners = partners + (time_count - 1)
+    for level in range(1, levels):
+        for delta in (-(1 << level), 1 << level):
+            there = (core == 0) & (line + delta >= 0) & (line + delta <= last)
+
+            @pl.when(there)
+            def _():
+                pl.semaphore_signal(
+                    barrier, inc=1, device_id=(line + delta, time), device_id_type=MESH
+                )
+
+            partners = partners + jnp.where(there, 1, 0)
+    pl.semaphore_wait(barrier, partners)
+
+    def remote(source, target, sems, to_line, to_time=None):
+        return pltpu.make_async_remote_copy(
+            src_ref=source,
+            dst_ref=target,
+            send_sem=sems[0],
+            recv_sem=sems[1],
+            device_id=(to_line, time if to_time is None else to_time),
+            device_id_type=MESH,
+        )
+
+    def span_copy():
+        return remote(span_ref.at[0], prev_span, (span_sems.at[0], span_sems.at[1]), line + 1)
+
+    def map_copy():
+        return remote(maps_ref.at[0, 1], prev_map, (map_sems.at[0], map_sems.at[1]), line + 1)
+
+    def vel_copy(window):
+        return remote(
+            vel_ref,
+            next_vel.at[window],
+            (vel_sems.at[0, window], vel_sems.at[1, window]),
+            line - 1,
+        )
+
+    def update_copy(level, side):
+        stride = jnp.left_shift(1, level)
+        return remote(
+            update_out.at[side],
+            update.at[level, 1 - side],
+            (update_sems.at[0, level, side], update_sems.at[1, level, 1 - side]),
+            line + (2 * side - 1) * stride,
+        )
+
+    def update_wait(level, side):
+        remote(
+            update_out.at[side],
+            update.at[level, side],
+            (update_sems.at[0, level, side], update_sems.at[1, level, side]),
+            line,
+        ).wait_recv()
+
+    def couple_copy(level, side):
+        stride = jnp.left_shift(1, level)
+        return remote(
+            couple_out,
+            couple.at[level + 1, 1 - side],
+            (couple_sems.at[0, level, side], couple_sems.at[1, level, 1 - side]),
+            line + (2 * side - 1) * stride,
+        )
+
+    def couple_wait(level, side):
+        remote(
+            couple_out,
+            couple.at[level + 1, side],
+            (couple_sems.at[0, level, side], couple_sems.at[1, level, side]),
+            line,
+        ).wait_recv()
+
+    def vec_copy(window, level, side):
+        stride = jnp.left_shift(1, level)
+        return remote(
+            vec_out.at[window, level, side],
+            vec_in.at[window, level, 1 - side],
+            (vec_sems.at[0, window, level, side], vec_sems.at[1, window, level, 1 - side]),
+            line + (2 * side - 1) * stride,
+        )
+
+    def vec_wait(window, level, side):
+        remote(
+            vec_out.at[window, level, side],
+            vec_in.at[window, level, side],
+            (vec_sems.at[0, window, level, side], vec_sems.at[1, window, level, side]),
+            line,
+        ).wait_recv()
+
+    def there(level, side):
+        stride = jnp.left_shift(1, level)
+        return (line - stride >= 0) if side == 0 else (line + stride <= last)
+
+    def sends(level):
+        return core == jnp.where(level == 0, 1, 0)
+
+    vel_ref[...] = vel_in[...]
+    disp_ref[...] = disp_in[...]
+    acc_ref[...] = acc_in[...]
+    bad_ref[...] = jnp.zeros_like(bad_ref)
+
+    @pl.when(core == 0)
+    def _():
+        span_copy().start()
+
+    @pl.when(line > 0)
+    def _():
+        vel_copy(0).start()
+
+    @pl.when(line < last)
+    def _():
+        map_copy().start()
+
+    @pl.when(line == last)
+    def _():
+        next_vel[...] = jnp.zeros_like(next_vel)
+
+    own_diag = jnp.where(eye_mask(order), accel_scale * to_column(mass_ref[...]), 0.0)
+    diag_ref[...] = span_ref[0] + own_diag
+
+    @pl.when(core == 1)
+    def _():
+        couple[0, 1] = -jnp.where(line < last, 1.0, 0.0) * span_ref[0]
+        span_copy().wait_recv()
+        diag_ref[...] = diag_ref[...] + prev_span[...]
+        couple[0, 0] = -prev_span[...]
+
+    def load_copy(window, turn):
+        step = 0 if turn < time_count else 1
+        return remote(
+            load_out.at[window],
+            load_in.at[window, step, time],
+            (load_send_sems.at[window, turn], load_recv_sems.at[window, step, time]),
+            line + step,
+            lax.rem(time + turn, time_count),
+        )
+
+    def load_wait(window, step, group):
+        remote(
+            load_out.at[window],
+            load_in.at[window, step, group],
+            (load_send_sems.at[window, 0], load_recv_sems.at[window, step, group]),
+            line,
+        ).wait_recv()
+
+    def begin_loads(window):
+        velocity_col = to_column(vel_ref[...])
+        next_col = to_column(next_vel[window])
+        interior = vec_mat(velocity_col, maps_ref[0, 0]) + vec_mat(next_col, maps_ref[0, 1])
+        offset = mean_ref[...] - interior
+        count, samples, width = wind_ref.shape
+
+        def add(group, total):
+            relative = wind_ref[group].astype(jnp.float32) + offset
+            return total + weight_ref[window, group] * (relative * jnp.abs(relative))
+
+        total = lax.fori_loop(0, count, add, jnp.zeros((samples, width), jnp.float32))
+        load = drag_ref[...] * jnp.sum(total, axis=0, keepdims=True) * window_scale
+        load_out[window] = load
+        load_in[window, 0, time] = load
+        for turn in range(1, time_count):
+            load_copy(window, turn).start()
+
+        @pl.when(line < last)
+        def _():
+            for turn in range(time_count, 2 * time_count):
+                load_copy(window, turn).start()
+
+    def end_loads(window):
+        for turn in range(1, time_count):
+            load_wait(window, 0, lax.rem(time + turn, time_count))
+
+        @pl.when(line > 0)
+        def _():
+            for turn in range(time_count):
+                load_wait(window, 1, lax.rem(time + turn, time_count))
+
+        def summed(step):
+            total = load_in[window, step, 0]
+            for group in range(1, time_count):
+                total = total + load_in[window, step, group]
+            return total
+
+        inertia = mass_ref[...] * (
+            accel_scale * disp_ref[...] + velocity_scale * vel_ref[...] + acc_ref[...]
+        )
+        side_ref[...] = inertia + to_row(mat_vec(maps_ref[0, 0], summed(0)))
+
+        @pl.when(line > 0)
+        def _():
+            if window == 0:
+                map_copy().wait_recv()
+            side_ref[...] = side_ref[...] + to_row(mat_vec(prev_map[...], summed(1)))
+
+    def reduce_vector(window, level):
+        @pl.when(sends(level))
+        def _():
+            column = to_column(side_ref[...])
+            for side in range(2):
+                vec_out[window, level, side, :, :order] = vec_mat(column, scaled[level, side])
+                vec_out[window, level, side, :, order:] = bad_ref[...]
+
+                @pl.when(there(level, side))
+                def _():
+                    vec_copy(window, level, side).start()
+
+        @pl.when(core == 0)
+        def _():
+            for side in range(2):
+
+                @pl.when(there(level, side))
+                def _():
+                    vec_wait(window, level, side)
+                    side_ref[...] = side_ref[...] - vec_in[window, level, side, :, :order]
+                    if window == 1:
+                        bad_ref[...] = bad_ref[...] + vec_in[window, level, side, :, order:]
+
+    def factor_level(level, carry):
+        @pl.when(sends(level))
+        def _():
+            newton_inverse(diag_ref, inverse_ref, bad_ref)
+
+        before = jnp.maximum(level - 1, 0)
+        for side in range(2):
+            expected = (level >= 1) & (level < levels) & (core == 0)
+
+            @pl.when(expected & there(before, side))
+            def _():
+                couple_wait(before, side)
+
+            @pl.when(expected & jnp.logical_not(there(before, side)))
+            def _():
+                couple[level, side] = jnp.zeros((order, order), jnp.float32)
+
+        for side in range(2):
+            sent = (level >= 1) & sends(before) & there(before, side)
+
+            @pl.when(sent)
+            def _():
+                update_copy(before, side).wait_send()
+
+            @pl.when(sent & (level < levels))
+            def _():
+                couple_copy(before, side).wait_send()
+
+        @pl.when(sends(level) & (level < levels))
+        def _():
+            inverse = inverse_ref[...]
+            scaled[level, 0] = split_dot(inverse, couple[level, 0], 1, 1)
+            update_out[0] = split_dot(couple[level, 0], scaled[level, 0])
+
+            @pl.when(there(level, 0))
+            def _():
+                update_copy(level, 0).start()
+
+            scaled[level, 1] = split_dot(inverse, couple[level, 1])
+            own = jnp.where(level == 0, 1.0, 0.0)
+            update_out[1] = split_dot(couple[level, 1], scaled[level, 1], 0, 0) - own * span_ref[0]
+
+            @pl.when(there(level, 1))
+            def _():
+                update_copy(level, 1).start()
+
+            @pl.when(level < levels - 1)
+            def _():
+                couple_out[...] = -split_dot(couple[level, 0], scaled[level, 1])
+                for side in range(2):
+
+                    @pl.when(there(level, side))
+                    def _():
+                        couple_copy(level, side).start()
+
+        @pl.when(level == 0)
+        def _():
+            @pl.when(line < last)
+            def _():
+                vel_wait(0)
+
+            begin_loads(0)
+            end_loads(0)
+
+        @pl.when(level < levels)
+        def _():
+            reduce_vector(0, level)
+
+            @pl.when(core == 0)
+            def _():
+                for side in range(2):
+
+                    @pl.when(there(level, side))
+                    def _():
+                        update_wait(level, side)
+                        diag_ref[...] = diag_ref[...] - update[level, side]
+
+        return carry
+
+    def vel_wait(window):
+        remote(
+            vel_ref,
+            next_vel.at[window],
+            (vel_sems.at[0, window], vel_sems.at[1, window]),
+            line,
+        ).wait_recv()
+
+    lax.fori_loop(0, levels + 1, factor_level, 0)
+
+    def sol_copy(window, side):
+        return remote(
+            sol_out.at[window],
+            sol_in.at[window, 1 - side],
+            (sol_sems.at[0, window, side], sol_sems.at[1, window, 1 - side]),
+            line + 2 * side - 1,
+        )
+
+    def sol_wait(window, side):
+        remote(
+            sol_out.at[window],
+            sol_in.at[window, side],
+            (sol_sems.at[0, window, side], sol_sems.at[1, window, side]),
+            line,
+        ).wait_recv()
+
+    def advance(solution_row):
+        new_accel = (
+            accel_scale * (solution_row - disp_ref[...])
+            - velocity_scale * vel_ref[...]
+            - acc_ref[...]
+        )
+        vel_ref[...] = vel_ref[...] + half_step * (acc_ref[...] + new_accel)
+        disp_ref[...] = solution_row
+        acc_ref[...] = new_accel
+
+    @pl.when(line > 0)
+    def _():
+        vel_copy(0).wait_send()
+
+    def finish(window):
+        @pl.when(core == 0)
+        def _():
+            advance(vec_mat(to_column(side_ref[...]), inverse_ref[...]))
+            sol_out[window, :, :order] = disp_ref[...]
+            sol_out[window, :, order : 2 * order] = vel_ref[...]
+            sol_out[window, :, 2 * order :] = bad_ref[...]
+            sol_copy(window, 1).start()
+
+            @pl.when(line > 0)
+            def _():
+                sol_copy(window, 0).start()
+
+        @pl.when(core == 1)
+        def _():
+            value = vec_mat(to_column(side_ref[...]), inverse_ref[...])
+            sol_wait(window, 0)
+            behind = mat_vec(scaled[0, 0], sol_in[window, 0, :, :order])
+            side_ref[...] = value - to_row(behind)
+            if window == 1:
+                bad_ref[...] = sol_in[window, 0, :, 2 * order :]
+
+            @pl.when(line < last)
+            def _():
+                sol_wait(window, 1)
+                ahead = mat_vec(scaled[0, 1], sol_in[window, 1, :, :order])
+                side_ref[...] = side_ref[...] - to_row(ahead)
+                if window == 0:
+                    next_vel[1] = sol_in[window, 1, :, order : 2 * order]
+
+            advance(side_ref[...])
+            if window == 0:
+                vel_copy(1).start()
+
+    finish(0)
+
+    @pl.when(core == 0)
+    def _():
+        vel_wait(1)
+
+    begin_loads(1)
+    end_loads(1)
+
+    def reduce_level(level, carry):
+        reduce_vector(1, level)
+        return carry
+
+    lax.fori_loop(0, levels, reduce_level, 0)
+
+    @pl.when(core == 1)
+    def _():
+        vel_copy(1).wait_send()
+
+    finish(1)
+    bad_out[...] = bad_ref[...]
+
+    @pl.when(core == 0)
+    def _():
+        span_copy().wait_send()
+
+    @pl.when(line < last)
+    def _():
+        map_copy().wait_send()
+
+    for window in range(2):
+        for turn in range(1, time_count):
+            load_copy(window, turn).wait_send()
+
+        @pl.when(line < last)
+        def _():
+            for turn in range(time_count, 2 * time_count):
+                load_copy(window, turn).wait_send()
+
+        @pl.when(core == 0)
+        def _():
+            sol_copy(window, 1).wait_send()
+
+            @pl.when(line > 0)
+            def _():
+                sol_copy(window, 0).wait_send()
+
+    def drain(level, carry):
+        for window in range(2):
+            for side in range(2):
+
+                @pl.when(sends(level) & there(level, side))
+                def _():
+                    vec_copy(window, level, side).wait_send()
+
+        return carry
+
+    lax.fori_loop(0, levels, drain, 0)
+
+
+def run_line(
+    line_count,
+    time_count,
+    window_scale,
+    weights,
+    arrived,
+    mean_wind,
+    drag,
+    transfer,
+    span_stiff,
+    mass,
+    disp0,
+    vel0,
+    acc0,
+):
+    order = span_stiff.shape[-1]
+    width = mean_wind.shape[-1]
+    levels = (line_count - 1).bit_length()
+    row = jax.ShapeDtypeStruct((1, order), jnp.float32)
+
+    def body(*refs):
+        line_kernel(line_count, time_count, window_scale, levels, *refs)
+
+    vmem = pl.BlockSpec(memory_space=pltpu.VMEM)
+    dma = pltpu.SemaphoreType.DMA
+
+    def buffer(*shape):
+        return pltpu.VMEM(shape, jnp.float32)
+
+    return pl.pallas_call(
+        body,
+        out_shape=(row, row, jax.ShapeDtypeStruct((1, LANES), jnp.float32)),
+        in_specs=[pl.BlockSpec(memory_space=pltpu.SMEM)] + [vmem] * 9,
+        out_specs=[vmem] * 3,
+        scratch_shapes=[
+            buffer(1, order),
+            buffer(1, LANES),
+            buffer(1, order),
+            buffer(order, order),
+            buffer(order, order),
+            buffer(order, order),
+            buffer(order, width),
+            buffer(2, 1, order),
+            buffer(levels, 2, order, order),
+            buffer(levels, 2, order, order),
+            buffer(levels, 2, order, order),
+            buffer(2, order, order),
+            buffer(order, order),
+            buffer(2, levels, 2, 1, order + LANES),
+            buffer(2, levels, 2, 1, order + LANES),
+            buffer(2, 1, width),
+            buffer(2, 2, time_count, 1, width),
+            buffer(2, 1, 2 * order + LANES),
+            buffer(2, 2, 1, 2 * order + LANES),
+            dma((2,)),
+            dma((2,)),
+            dma((2, 2)),
+            dma((2, levels, 2)),
+            dma((2, levels, 2)),
+            dma((2, 2, levels, 2)),
+            dma((2, 2 * time_count)),
+            dma((2, 2, time_count)),
+            dma((2, 2, 2)),
+        ],
+        compiler_params=pltpu.CompilerParams(
+            collective_id=0, has_side_effects=True, vmem_limit_bytes=60 * 2**20
+        ),
+        cost_estimate=pl.CostEstimate(
+            flops=100 * order**3, bytes_accessed=5 * 2**20, transcendentals=0
+        ),
+    )(weights, arrived, mean_wind, drag, transfer, span_stiff, mass, disp0, vel0, acc0)
+
+
+def local(
+    gust_coef,
+    mean_wind,
+    drag,
+    span_column,
+    segment_step,
+    transfer,
+    span_stiff,
+    mass,
+    disp0,
+    vel0,
+    acc0,
+):
+    line_count = lax.axis_size("line")
+    time_count = lax.axis_size("tm")
+    time_pos = lax.axis_index("tm")
+    span_count = span_column.shape[0]
+    seg_count = segment_step.shape[0]
+    trig_rows = trig_table(TS, KF)
+    spectra = gust_coef.reshape(2 * KF, span_count * Q)
+    wind_field = jnp.dot(trig_rows, spectra, preferred_element_type=jnp.float32).astype(
+        jnp.bfloat16
+    )
+    wind_field = jnp.take(wind_field.reshape(TS, span_count, Q), span_column, axis=1)
+    window_scale = 1.0 / (TS * (seg_count // 2))
+    arrived = lax.all_to_all(wind_field, "line", split_axis=1, concat_axis=0, tiled=True)
+    arrived = arrived.reshape(line_count, TS, Q)
+    seg_index = jnp.arange(line_count, dtype=jnp.int32) * time_count + time_pos
+    seg_flags = jnp.take(segment_step, seg_index)
+    weights = (seg_flags[None] == jnp.arange(2, dtype=jnp.int32)[:, None]).astype(jnp.float32)
+    fast_disp, fast_vel, bad = run_line(
+        line_count,
+        time_count,
+        window_scale,
+        weights,
+        arrived,
+        mean_wind,
+        drag,
+        transfer,
+        span_stiff,
+        mass,
+        disp0,
+        vel0,
+        acc0,
+    )
+
+    def checked():
+        return checked_loop(
+            line_count,
+            time_count,
+            arrived,
+            seg_flags,
+            mean_wind,
+            drag,
+            transfer,
+            span_stiff,
+            mass,
+            disp0,
+            vel0,
+            acc0,
+            window_scale,
+        )
+
+    return lax.cond(bad[0, 0] < 0.5, lambda: (fast_disp, fast_vel), checked)
+
+
 def solution(mesh):
     return jax.shard_map(
         local,

time: 1580 us -> 257 us (0.16); the launches traced: 1560 us -> 256 us
  other arithmetic: 807 us -> 3.23 us
  matrix products: 244 us -> 0.49 us
  Pallas kernels: 0 us -> 220 us
  waiting for transfers between devices: 197 us -> 15.6 us
  local copies, waits for them, and re-layouts: 151 us -> 7 us
  starting transfers between devices: 143 us -> 8.59 us
  blocking collectives: 16 us -> 0 us
    another operation x138 -> x1, other arithmetic: 774 us -> 0.15 us  [the longest x72 305 us: blocked_cholesky(): corner = jnp.linalg.cholesky(trailing[start_row:end_row, start_row:end_row])]
    pallas_call x0 -> x1, Pallas kernels: none -> 220 us  [run_line(): pl.pallas_call(body, out_shape=(row, row, jax.ShapeDtypeStruct((1, LANES)...]
    ppermute x35 -> x0, waiting for transfers between devices: 189 us -> none  [shifted(): return lax.ppermute(array, axis, pairs)]
    another operation x256 -> x0, matrix products: 137 us -> none  [the longest x238 118 us: cho_apply(): return jax.scipy.linalg.cho_solve((factor, True), values)]
    ppermute x35 -> x0, starting transfers between devices: 136 us -> none  [shifted(): return lax.ppermute(array, axis, pairs)]
    dot_general x64 -> x0, matrix products: 107 us -> none  [exact_dot(): jnp.dot(first, second, precision=lax.Precision.HIGHEST, preferred_element...]
    another operation x97 -> x0, local copies, waits for them, and re-layouts: 87.4 us -> none  [the longest x79 75.6 us: cho_apply(): return jax.scipy.linalg.cho_solve((factor, True), values)]
    scatter x24 -> x0, local copies, waits for them, and re-layouts: 26.5 us -> none  [the longest x18 20 us: blocked_cholesky(): factor = factor.at[end_row:, start_row:end_row].set(below_factor)]
  transfers between devices with their start and end apart: 36 -> 1, of which waited for: 13 -> 1; matrix products, arithmetic and copies ran while one was open for 4% -> 1% of each run, Pallas kernels for 0% -> 0%
where the time goes in v2:
time: 257 us; the launch traced here: 256 us
  Pallas kernels  220 us (86%)
  waiting for transfers between devices  15.6 us (6%)
  starting transfers between devices  8.59 us (3%)
  local copies, waits for them, and re-layouts  7 us (3%)
  other arithmetic  3.23 us (1%)
    pallas_call x1, Pallas kernels, run_line(): pl.pallas_call(body, out_shape=(row, row, jax.ShapeDtypeStruct((1, LANES)...  220 us
    all_to_all x1, waiting for transfers between devices, local(): lax.all_to_all(wind_field, 'line', split_axis=1, concat_axis=0, tiled=True)  15.6 us
    all_to_all x1, starting transfers between devices, local(): lax.all_to_all(wind_field, 'line', split_axis=1, concat_axis=0, tiled=True)  8.59 us
    unnamed x21, local copies, waits for them, and re-layouts  5.57 us
  transfers between devices with their start and end apart: 1, of which 1 were waited for; matrix products, arithmetic and copies ran while one was open for 1% of the time, Pallas kernels for 0%

profile of v2, /device:TPU:1, one launch (start us, length us, event | category | flops | bytes accessed | tf_op | source)
XLA Modules:
  0.0 256.4 jit_solution(7838680009273288488)
XLA Ops:
  0.6 0.0 copy-start
  0.7 0.7 compare_select_fusion
  1.3 0.7 compare_and_fusion
  2.0 3.0 %copy.186 = bf16[16,8,32,256]{3,1,2,0:T(8,128)(2,1)S(1)} copy(bf16[16,8,32,256]{3,2,1,0:T(8,128)(2,1)} %bitcast.1812) | data formatting | bytes 4194304
  5.0 0.1 cosine_convert_fusion
  5.1 0.5 convolution_convert_fusion
  5.6 0.1 copy.188
  5.8 0.6 gather_fusion.1
  6.4 0.0 copy-start.20
  6.4 0.0 copy-start.61
  6.4 0.0 copy-start.62
  6.4 0.0 copy-start.65
  6.5 0.0 copy-start.68
  6.5 0.0 copy-start.71
  6.5 0.0 copy-start.74
  6.5 1.2 select_bitcast_fusion.3
  7.6 8.6 %all-to-all-start = ((bf16[64,32,256]{2,0,1:T(8,128)(2,1)}), bf16[64,32,256]{2,0,1:T(8,128)(2,1)S(1)}, u32[]{:S(2)}, u32[]{:S(2)}) async-start(bf16[64,32,256]{2,0,1:T(8,128)(2,1)} %select_bitcast_fusion.3), calls=%async_computation | async-start | bytes 2097152 | tf_op jit(solution)/shard_map/all_to_all | solution.py:827
  16.3 0.0 copy-done
  16.3 0.7 gather_fusion
  17.0 0.6 compare_convert_fusion.2.refs_0_
  17.6 15.6 %all-to-all-done = bf16[64,32,256]{2,0,1:T(8,128)(2,1)S(1)} async-done(((bf16[64,32,256]{2,0,1:T(8,128)(2,1)}), bf16[64,32,256]{2,0,1:T(8,128)(2,1)S(1)}, u32[]{:S(2)}, u32[]{:S(2)}) %all-to-all-start) | async-done | bytes 1048608 | tf_op jit(solution)/shard_map/all_to_all | solution.py:827
  33.1 0.0 copy-done.20
  33.2 0.0 copy-done.61
  33.2 0.0 copy-done.65
  33.2 0.0 copy-done.68
  33.2 0.0 copy-done.71
  33.2 0.0 copy-done.74
  33.2 219.8 %shard_map.126 = (f32[1,512]{1,0:T(1,128)}, f32[1,512]{1,0:T(1,128)}, f32[1,128]{1,0:T(1,128)}) custom-call(f32[2,32]{1,0:T(2,128)} %compare_convert_fusion.2.refs_0_, bf16[32,64,256]{2,1,0:T(8,128)(2,1)S(1)} %bitcast.1806, f32[1,256]{1,0:T(1,128)S(1)} %copy-done.74, f32[1,256]{1,0:T(1,128)S(1)} %copy-done.65, f32[1,2,512,256]{3,2,1,0:T(8,128)S(1)} %copy-done.20, ...), custom_call_target="tpu_custom_call" | custom-call | flops 13421772800 | bytes 5242880 | tf_op jit(solution)/shard_map/pallas_call | solution.py:758
  253.7 0.3 conditional.1
  253.9 0.0 copy-start.1
  253.9 1.3 copy.281
  255.2 1.2 copy.282
  (7 shorter events, 0.0 us)
Async XLA Ops:
  0.6 15.6 %copy-start = (s32[128]{0:T(128)S(1)}, s32[128]{0:T(128)}, u32[]{:S(2)}) copy-start(s32[128]{0:T(128)} %param.148) | copy-start | bytes 1540
  6.4 26.7 %copy-start.20 = (f32[1,2,512,256]{3,2,1,0:T(8,128)S(1)}, f32[1,2,512,256]{3,2,1,0:T(8,128)}, u32[]{:S(2)}) copy-start(f32[1,2,512,256]{3,2,1,0:T(8,128)} %refs_4_.1) | copy-start | bytes 3145732
  6.4 26.7 %copy-start.61 = (f32[1,512]{1,0:T(1,128)S(1)}, f32[1,512]{1,0:T(1,128)}, u32[]{:S(2)}) copy-start(f32[1,512]{1,0:T(1,128)} %refs_8_.1) | copy-start | bytes 6148
  6.4 26.7 %copy-start.62 = (f32[1,512]{1,0:T(1,128)S(1)}, f32[1,512]{1,0:T(1,128)}, u32[]{:S(2)}) copy-start(f32[1,512]{1,0:T(1,128)} %refs_6_.1) | copy-start | bytes 6148
  6.4 26.7 %copy-start.65 = (f32[1,256]{1,0:T(1,128)S(1)}, f32[1,256]{1,0:T(1,128)}, u32[]{:S(2)}) copy-start(f32[1,256]{1,0:T(1,128)} %refs_3_.1) | copy-start | bytes 3076
  6.5 26.7 %copy-start.68 = (f32[1,512]{1,0:T(1,128)S(1)}, f32[1,512]{1,0:T(1,128)}, u32[]{:S(2)}) copy-start(f32[1,512]{1,0:T(1,128)} %refs_7_.1) | copy-start | bytes 6148
  6.5 26.7 %copy-start.71 = (f32[1,512]{1,0:T(1,128)S(1)}, f32[1,512]{1,0:T(1,128)}, u32[]{:S(2)}) copy-start(f32[1,512]{1,0:T(1,128)} %refs_9_.1) | copy-start | bytes 6148
  6.5 26.7 %copy-start.74 = (f32[1,256]{1,0:T(1,128)S(1)}, f32[1,256]{1,0:T(1,128)}, u32[]{:S(2)}) copy-start(f32[1,256]{1,0:T(1,128)} %refs_2_.1) | copy-start | bytes 3076
  7.6 25.5 %all-to-all-start = ((bf16[64,32,256]{2,0,1:T(8,128)(2,1)}), bf16[64,32,256]{2,0,1:T(8,128)(2,1)S(1)}, u32[]{:S(2)}, u32[]{:S(2)}) async-start(bf16[64,32,256]{2,0,1:T(8,128)(2,1)} %select_bitcast_fusion.3), calls=%async_computation | async-start | bytes 2097152 | tf_op jit(solution)/shard_map/all_to_all | solution.py:827
  253.9 2.5 copy-start.1

commit v3 on v2

--- a/solution.py
+++ b/solution.py
@@ -196,7 +196,7 @@
     return jnp.sum(matrix * row, axis=1, keepdims=True)
 
 
-def newton_inverse(diag_ref, inverse_ref, bad_ref, bound_on_residual=9e-6):
+def newton_inverse(diag_ref, inverse_ref, bad_ref, bound_on_residual=0.03):
     order = diag_ref.shape[0]
     mask = eye_mask(order)
     diag = diag_ref[...]
@@ -211,13 +211,21 @@
     inverse_ref[...] = (scale / diag_col) * (2.0 * identity - diag * (scale / diag_row))
     current = inverse_ref[...]
     residual = identity - single_dot(diag_ref[...], current)
-    inverse_ref[...] = current + single_dot(current, residual)
-    for _ in range(2):
-        current = inverse_ref[...]
-        residual = identity - split_dot(diag_ref[...], current)
-        inverse_ref[...] = current + single_dot(current, residual)
-    size = jnp.sum(jnp.sum(residual * residual, axis=0, keepdims=True), axis=1, keepdims=True)
+    estimate = (current + single_dot(current, residual)).astype(jnp.bfloat16)
+    diag_hi, diag_lo = halves(diag_ref[...])
+    residual = (
+        identity
+        - jnp.dot(diag_hi, estimate, preferred_element_type=jnp.float32)
+        - jnp.dot(diag_lo, estimate, preferred_element_type=jnp.float32)
+    )
+    size = jnp.max(jnp.sum(jnp.abs(residual), axis=0, keepdims=True), axis=1, keepdims=True)
     bad_ref[...] = bad_ref[...] + jnp.where(size < bound_on_residual, 0.0, 1.0)
+    series_hi, series_lo = halves(residual + single_dot(residual, residual))
+    inverse_ref[...] = (
+        estimate.astype(jnp.float32)
+        + jnp.dot(estimate, series_hi, preferred_element_type=jnp.float32)
+        + jnp.dot(estimate, series_lo, preferred_element_type=jnp.float32)
+    )
 
 
 def line_kernel(
@@ -262,6 +270,8 @@
     vel_sems,
     update_sems,
     couple_sems,
+    share_send_sems,
+    share_recv_sems,
     vec_sems,
     load_send_sems,
     load_recv_sems,
@@ -334,28 +344,45 @@
             line - 1,
         )
 
-    def update_copy(level, side):
+    blocks = order // LANES
+    quarter = order // time_count
+
+    def triangle(ref, block):
+        start = block * LANES
+        return ref.at[pl.ds(start, LANES), pl.ds(start, order - start)]
+
+    def own_rows(ref, group):
+        return ref.at[pl.ds(pl.multiple_of(group * quarter, quarter), quarter)]
+
+    def update_copies(level, side):
         stride = jnp.left_shift(1, level)
-        return remote(
-            update_out.at[side],
-            update.at[level, 1 - side],
-            (update_sems.at[0, level, side], update_sems.at[1, level, 1 - side]),
-            line + (2 * side - 1) * stride,
-        )
+        return [
+            remote(
+                triangle(update_out.at[side], block),
+                triangle(update.at[level, 1 - side], block),
+                (
+                    update_sems.at[0, level, side, block],
+                    update_sems.at[1, level, 1 - side, block],
+                ),
+                line + (2 * side - 1) * stride,
+            )
+            for block in range(blocks)
+        ]
 
     def update_wait(level, side):
-        remote(
-            update_out.at[side],
-            update.at[level, side],
-            (update_sems.at[0, level, side], update_sems.at[1, level, side]),
-            line,
-        ).wait_recv()
+        for block in range(blocks):
+            remote(
+                triangle(update_out.at[side], block),
+                triangle(update.at[level, side], block),
+                (update_sems.at[0, level, side, block], update_sems.at[1, level, side, block]),
+                line,
+            ).wait_recv()
 
     def couple_copy(level, side):
         stride = jnp.left_shift(1, level)
         return remote(
             couple_out,
-            couple.at[level + 1, 1 - side],
+            own_rows(couple.at[level + 1, 1 - side], time),
             (couple_sems.at[0, level, side], couple_sems.at[1, level, 1 - side]),
             line + (2 * side - 1) * stride,
         )
@@ -363,8 +390,28 @@
     def couple_wait(level, side):
         remote(
             couple_out,
-            couple.at[level + 1, side],
+            own_rows(couple.at[level + 1, side], time),
             (couple_sems.at[0, level, side], couple_sems.at[1, level, side]),
+            line,
+        ).wait_recv()
+
+    def share_copy(level, side, turn):
+        rows = own_rows(couple.at[level + 1, side], time)
+        return remote(
+            rows,
+            rows,
+            (share_send_sems.at[level, side, turn], share_recv_sems.at[level, side, time]),
+            line,
+            lax.rem(time + turn, time_count),
+        )
+
+    def share_wait(level, side, turn):
+        group = lax.rem(time + turn, time_count)
+        rows = own_rows(couple.at[level + 1, side], group)
+        remote(
+            rows,
+            rows,
+            (share_send_sems.at[level, side, turn], share_recv_sems.at[level, side, group]),
             line,
         ).wait_recv()
 
@@ -519,55 +566,64 @@
             newton_inverse(diag_ref, inverse_ref, bad_ref)
 
         before = jnp.maximum(level - 1, 0)
-        for side in range(2):
-            expected = (level >= 1) & (level < levels) & (core == 0)
-
-            @pl.when(expected & there(before, side))
-            def _():
-                couple_wait(before, side)
-
-            @pl.when(expected & jnp.logical_not(there(before, side)))
-            def _():
-                couple[level, side] = jnp.zeros((order, order), jnp.float32)
 
         for side in range(2):
             sent = (level >= 1) & sends(before) & there(before, side)
 
             @pl.when(sent)
             def _():
-                update_copy(before, side).wait_send()
+                for copy in update_copies(before, side):
+                    copy.wait_send()
 
             @pl.when(sent & (level < levels))
             def _():
                 couple_copy(before, side).wait_send()
 
+        def coupling(side):
+            expected = (level >= 1) & (core == 0)
+
+            @pl.when(expected & there(before, side))
+            def _():
+                for turn in range(1, time_count):
+                    share_wait(before, side, turn)
+                    share_copy(before, side, turn).wait_send()
+
+            @pl.when(expected & jnp.logical_not(there(before, side)))
+            def _():
+                couple[level, side] = jnp.zeros((order, order), jnp.float32)
+
         @pl.when(sends(level) & (level < levels))
         def _():
-            inverse = inverse_ref[...]
-            scaled[level, 0] = split_dot(inverse, couple[level, 0], 1, 1)
-            update_out[0] = split_dot(couple[level, 0], scaled[level, 0])
-
-            @pl.when(there(level, 0))
-            def _():
-                update_copy(level, 0).start()
-
-            scaled[level, 1] = split_dot(inverse, couple[level, 1])
-            own = jnp.where(level == 0, 1.0, 0.0)
-            update_out[1] = split_dot(couple[level, 1], scaled[level, 1], 0, 0) - own * span_ref[0]
-
-            @pl.when(there(level, 1))
-            def _():
-                update_copy(level, 1).start()
+            coupling(0)
+            scaled[level, 0] = split_dot(inverse_ref[...], couple[level, 0], 1, 1)
+            coupling(1)
+            scaled[level, 1] = split_dot(inverse_ref[...], couple[level, 1])
 
             @pl.when(level < levels - 1)
             def _():
-                couple_out[...] = -split_dot(couple[level, 0], scaled[level, 1])
+                rows = pl.ds(pl.multiple_of(time * quarter, quarter), quarter)
+                couple_out[...] = -split_dot(couple[level, 0, rows], scaled[level, 1])
                 for side in range(2):
 
                     @pl.when(there(level, side))
                     def _():
                         couple_copy(level, side).start()
 
+            update_out[0] = split_dot(couple[level, 0], scaled[level, 0])
+
+            @pl.when(there(level, 0))
+            def _():
+                for copy in update_copies(level, 0):
+                    copy.start()
+
+            own = jnp.where(level == 0, 1.0, 0.0)
+            update_out[1] = split_dot(couple[level, 1], scaled[level, 1], 0, 0) - own * span_ref[0]
+
+            @pl.when(there(level, 1))
+            def _():
+                for copy in update_copies(level, 1):
+                    copy.start()
+
         @pl.when(level == 0)
         def _():
             @pl.when(line < last)
@@ -575,6 +631,17 @@
                 vel_wait(0)
 
             begin_loads(0)
+
+        for side in range(2):
+
+            @pl.when((level < levels - 1) & (core == 0) & there(level, side))
+            def _():
+                couple_wait(level, side)
+                for turn in range(1, time_count):
+                    share_copy(level, side, turn).start()
+
+        @pl.when(level == 0)
+        def _():
             end_loads(0)
 
         @pl.when(level < levels)
@@ -588,7 +655,16 @@
                     @pl.when(there(level, side))
                     def _():
                         update_wait(level, side)
-                        diag_ref[...] = diag_ref[...] - update[level, side]
+                        for block in range(blocks):
+                            start = block * LANES
+                            part = (pl.ds(start, LANES), pl.ds(start, order - start))
+                            diag_ref[part] = diag_ref[part] - update[(level, side) + part]
+
+                for block in range(blocks):
+                    rows = pl.ds(block * LANES, LANES)
+                    for other in range(block + 1, blocks):
+                        columns = pl.ds(other * LANES, LANES)
+                        diag_ref[columns, rows] = diag_ref[rows, columns].T
 
         return carry
 
@@ -773,7 +849,7 @@
             buffer(levels, 2, order, order),
             buffer(levels, 2, order, order),
             buffer(2, order, order),
-            buffer(order, order),
+            buffer(order // time_count, order),
             buffer(2, levels, 2, 1, order + LANES),
             buffer(2, levels, 2, 1, order + LANES),
             buffer(2, 1, width),
@@ -783,8 +859,10 @@
             dma((2,)),
             dma((2,)),
             dma((2, 2)),
+            dma((2, levels, 2, order // LANES)),
             dma((2, levels, 2)),
-            dma((2, levels, 2)),
+            dma((levels, 2, time_count)),
+            dma((levels, 2, time_count)),
             dma((2, 2, levels, 2)),
             dma((2, 2 * time_count)),
             dma((2, 2, time_count)),

time: 257 us -> 193 us (0.75)
  Pallas kernels: 220 us -> 156 us
    pallas_call x1, Pallas kernels: 220 us -> 156 us  [run_line(): pl.pallas_call(body, out_shape=(row, row, jax.ShapeDtypeStruct((1, LANES)...]
where the time goes in v3:
time: 193 us
  Pallas kernels  156 us (81%)
  waiting for transfers between devices  15.6 us (8%)
  starting transfers between devices  8.59 us (4%)
  local copies, waits for them, and re-layouts  7 us (4%)
  other arithmetic  3.23 us (2%)
    pallas_call x1, Pallas kernels, run_line(): pl.pallas_call(body, out_shape=(row, row, jax.ShapeDtypeStruct((1, LANES)...  156 us
    all_to_all x1, waiting for transfers between devices, local(): lax.all_to_all(wind_field, 'line', split_axis=1, concat_axis=0, tiled=True)  15.6 us
    all_to_all x1, starting transfers between devices, local(): lax.all_to_all(wind_field, 'line', split_axis=1, concat_axis=0, tiled=True)  8.59 us
    unnamed x21, local copies, waits for them, and re-layouts  5.57 us
  transfers between devices with their start and end apart: 1, of which 1 were waited for; matrix products, arithmetic and copies ran while one was open for 1% of the time, Pallas kernels for 0%

profile of v3, /device:TPU:1, one launch (start us, length us, event | category | flops | bytes accessed | tf_op | source)
XLA Modules:
  0.0 192.6 jit_solution(17120984066151029351)
XLA Ops:
  0.6 0.0 copy-start
  0.7 0.7 compare_select_fusion
  1.3 0.7 compare_and_fusion
  2.0 3.0 %copy.186 = bf16[16,8,32,256]{3,1,2,0:T(8,128)(2,1)S(1)} copy(bf16[16,8,32,256]{3,2,1,0:T(8,128)(2,1)} %bitcast.1812) | data formatting | bytes 4194304
  5.0 0.1 cosine_convert_fusion
  5.1 0.5 convolution_convert_fusion
  5.6 0.1 copy.188
  5.8 0.6 gather_fusion.1
  6.4 0.0 copy-start.20
  6.4 0.0 copy-start.61
  6.4 0.0 copy-start.62
  6.4 0.0 copy-start.65
  6.5 0.0 copy-start.68
  6.5 0.0 copy-start.71
  6.5 0.0 copy-start.74
  6.5 1.2 select_bitcast_fusion.3
  7.6 8.6 %all-to-all-start = ((bf16[64,32,256]{2,0,1:T(8,128)(2,1)}), bf16[64,32,256]{2,0,1:T(8,128)(2,1)S(1)}, u32[]{:S(2)}, u32[]{:S(2)}) async-start(bf16[64,32,256]{2,0,1:T(8,128)(2,1)} %select_bitcast_fusion.3), calls=%async_computation | async-start | bytes 2097152 | tf_op jit(solution)/shard_map/all_to_all | solution.py:905
  16.3 0.0 copy-done
  16.3 0.7 gather_fusion
  17.0 0.6 compare_convert_fusion.2.refs_0_
  17.6 15.6 %all-to-all-done = bf16[64,32,256]{2,0,1:T(8,128)(2,1)S(1)} async-done(((bf16[64,32,256]{2,0,1:T(8,128)(2,1)}), bf16[64,32,256]{2,0,1:T(8,128)(2,1)S(1)}, u32[]{:S(2)}, u32[]{:S(2)}) %all-to-all-start) | async-done | bytes 1048608 | tf_op jit(solution)/shard_map/all_to_all | solution.py:905
  33.1 0.0 copy-done.20
  33.2 0.0 copy-done.65
  33.2 0.0 copy-done.68
  33.2 0.0 copy-done.71
  33.2 0.0 copy-done.74
  33.2 155.9 %shard_map.126 = (f32[1,512]{1,0:T(1,128)}, f32[1,512]{1,0:T(1,128)}, f32[1,128]{1,0:T(1,128)}) custom-call(f32[2,32]{1,0:T(2,128)} %compare_convert_fusion.2.refs_0_, bf16[32,64,256]{2,1,0:T(8,128)(2,1)S(1)} %bitcast.1806, f32[1,256]{1,0:T(1,128)S(1)} %copy-done.74, f32[1,256]{1,0:T(1,128)S(1)} %copy-done.65, f32[1,2,512,256]{3,2,1,0:T(8,128)S(1)} %copy-done.20, ...), custom_call_target="tpu_custom_call" | custom-call | flops 13421772800 | bytes 5242880 | tf_op jit(solution)/shard_map/pallas_call | solution.py:834
  189.8 0.3 conditional.1
  190.1 0.0 copy-start.1
  190.1 1.3 copy.281
  191.3 1.2 copy.282
  192.6 0.0 copy-done.1
  (7 shorter events, 0.0 us)
Async XLA Ops:
  0.6 15.6 %copy-start = (s32[128]{0:T(128)S(1)}, s32[128]{0:T(128)}, u32[]{:S(2)}) copy-start(s32[128]{0:T(128)} %param.148) | copy-start | bytes 1540
  6.4 26.7 %copy-start.20 = (f32[1,2,512,256]{3,2,1,0:T(8,128)S(1)}, f32[1,2,512,256]{3,2,1,0:T(8,128)}, u32[]{:S(2)}) copy-start(f32[1,2,512,256]{3,2,1,0:T(8,128)} %refs_4_.1) | copy-start | bytes 3145732
  6.4 26.7 %copy-start.61 = (f32[1,512]{1,0:T(1,128)S(1)}, f32[1,512]{1,0:T(1,128)}, u32[]{:S(2)}) copy-start(f32[1,512]{1,0:T(1,128)} %refs_8_.1) | copy-start | bytes 6148
  6.4 26.7 %copy-start.62 = (f32[1,512]{1,0:T(1,128)S(1)}, f32[1,512]{1,0:T(1,128)}, u32[]{:S(2)}) copy-start(f32[1,512]{1,0:T(1,128)} %refs_6_.1) | copy-start | bytes 6148
  6.4 26.7 %copy-start.65 = (f32[1,256]{1,0:T(1,128)S(1)}, f32[1,256]{1,0:T(1,128)}, u32[]{:S(2)}) copy-start(f32[1,256]{1,0:T(1,128)} %refs_3_.1) | copy-start | bytes 3076
  6.5 26.7 %copy-start.68 = (f32[1,512]{1,0:T(1,128)S(1)}, f32[1,512]{1,0:T(1,128)}, u32[]{:S(2)}) copy-start(f32[1,512]{1,0:T(1,128)} %refs_7_.1) | copy-start | bytes 6148
  6.5 26.7 %copy-start.71 = (f32[1,512]{1,0:T(1,128)S(1)}, f32[1,512]{1,0:T(1,128)}, u32[]{:S(2)}) copy-start(f32[1,512]{1,0:T(1,128)} %refs_9_.1) | copy-start | bytes 6148
  6.5 26.7 %copy-start.74 = (f32[1,256]{1,0:T(1,128)S(1)}, f32[1,256]{1,0:T(1,128)}, u32[]{:S(2)}) copy-start(f32[1,256]{1,0:T(1,128)} %refs_2_.1) | copy-start | bytes 3076
  7.6 25.5 %all-to-all-start = ((bf16[64,32,256]{2,0,1:T(8,128)(2,1)}), bf16[64,32,256]{2,0,1:T(8,128)(2,1)S(1)}, u32[]{:S(2)}, u32[]{:S(2)}) async-start(bf16[64,32,256]{2,0,1:T(8,128)(2,1)} %select_bitcast_fusion.3), calls=%async_computation | async-start | bytes 2097152 | tf_op jit(solution)/shard_map/all_to_all | solution.py:905
  190.1 2.5 %copy-start.1 = (s32[128]{0:T(128)S(1)}, s32[128]{0:T(128)}, u32[]{:S(2)}) copy-start(s32[128]{0:T(128)} %param.148) | copy-start | bytes 1540

commit v4 on v3

--- a/solution.py
+++ b/solution.py
@@ -234,7 +234,7 @@
     window_scale,
     levels,
     weight_ref,
-    wind_ref,
+    sent_ref,
     mean_ref,
     drag_ref,
     maps_ref,
@@ -276,6 +276,8 @@
     load_send_sems,
     load_recv_sems,
     sol_sems,
+    wind_ref,
+    wind_sems,
 ):
     line = lax.axis_index("line")
     time = lax.axis_index("tm")
@@ -287,7 +289,7 @@
     partners = jnp.int32(0)
     for delta in (-1, 1):
         there = (line + delta >= 0) & (line + delta <= last)
-        for turn in range(time_count):
+        for turn in range(1, time_count):
 
             @pl.when(there)
             def _():
@@ -298,7 +300,7 @@
                     device_id_type=MESH,
                 )
 
-        partners = partners + jnp.where(there, time_count, 0)
+        partners = partners + jnp.where(there, time_count - 1, 0)
     for turn in range(1, time_count):
         pl.semaphore_signal(
             barrier,
@@ -307,17 +309,18 @@
             device_id_type=MESH,
         )
     partners = partners + (time_count - 1)
-    for level in range(1, levels):
-        for delta in (-(1 << level), 1 << level):
-            there = (core == 0) & (line + delta >= 0) & (line + delta <= last)
-
-            @pl.when(there)
-            def _():
-                pl.semaphore_signal(
-                    barrier, inc=1, device_id=(line + delta, time), device_id_type=MESH
-                )
-
-            partners = partners + jnp.where(there, 1, 0)
+
+    def greet(turn, carry):
+        pl.semaphore_signal(
+            barrier,
+            inc=1,
+            device_id=(lax.rem(line + turn, line_count), time),
+            device_id_type=MESH,
+        )
+        return carry
+
+    lax.fori_loop(1, line_count, greet, 0)
+    partners = partners + (line_count - 1)
     pl.semaphore_wait(barrier, partners)
 
     def remote(source, target, sems, to_line, to_time=None):
@@ -460,6 +463,39 @@
     def _():
         next_vel[...] = jnp.zeros_like(next_vel)
 
+    def wind_copy(turn):
+        to_line = lax.rem(line + turn, line_count)
+        return remote(
+            sent_ref.at[to_line],
+            wind_ref.at[line],
+            (wind_sems.at[0, to_line], wind_sems.at[1, line]),
+            to_line,
+        )
+
+    def wind_wait(turn):
+        from_line = lax.rem(line + turn, line_count)
+        remote(
+            sent_ref.at[from_line],
+            wind_ref.at[from_line],
+            (wind_sems.at[0, from_line], wind_sems.at[1, from_line]),
+            from_line,
+        ).wait_recv()
+
+    def wind_start(turn, carry):
+        wind_copy(turn).start()
+        return carry
+
+    def wind_done(turn, carry):
+        wind_wait(turn)
+        return carry
+
+    def wind_left(turn, carry):
+        wind_copy(turn).wait_send()
+        return carry
+
+    lax.fori_loop(1, line_count, wind_start, 0)
+    wind_ref[line] = sent_ref[line]
+
     own_diag = jnp.where(eye_mask(order), accel_scale * to_column(mass_ref[...]), 0.0)
     diag_ref[...] = span_ref[0] + own_diag
 
@@ -630,6 +666,7 @@
             def _():
                 vel_wait(0)
 
+            lax.fori_loop(1, line_count, wind_done, 0)
             begin_loads(0)
 
         for side in range(2):
@@ -764,6 +801,8 @@
     finish(1)
     bad_out[...] = bad_ref[...]
 
+    lax.fori_loop(1, line_count, wind_left, 0)
+
     @pl.when(core == 0)
     def _():
         span_copy().wait_send()
@@ -807,7 +846,7 @@
     time_count,
     window_scale,
     weights,
-    arrived,
+    wind_field,
     mean_wind,
     drag,
     transfer,
@@ -867,6 +906,8 @@
             dma((2, 2 * time_count)),
             dma((2, 2, time_count)),
             dma((2, 2, 2)),
+            pltpu.VMEM(wind_field.shape, wind_field.dtype),
+            dma((2, line_count)),
         ],
         compiler_params=pltpu.CompilerParams(
             collective_id=0, has_side_effects=True, vmem_limit_bytes=60 * 2**20
@@ -874,7 +915,7 @@
         cost_estimate=pl.CostEstimate(
             flops=100 * order**3, bytes_accessed=5 * 2**20, transcendentals=0
         ),
-    )(weights, arrived, mean_wind, drag, transfer, span_stiff, mass, disp0, vel0, acc0)
+    )(weights, wind_field, mean_wind, drag, transfer, span_stiff, mass, disp0, vel0, acc0)
 
 
 def local(
@@ -900,19 +941,18 @@
     wind_field = jnp.dot(trig_rows, spectra, preferred_element_type=jnp.float32).astype(
         jnp.bfloat16
     )
-    wind_field = jnp.take(wind_field.reshape(TS, span_count, Q), span_column, axis=1)
+    wind_field = wind_field.reshape(TS, span_count, Q)
+    wind_field = wind_field.at[:, span_column].get(mode="promise_in_bounds").transpose(1, 0, 2)
     window_scale = 1.0 / (TS * (seg_count // 2))
-    arrived = lax.all_to_all(wind_field, "line", split_axis=1, concat_axis=0, tiled=True)
-    arrived = arrived.reshape(line_count, TS, Q)
     seg_index = jnp.arange(line_count, dtype=jnp.int32) * time_count + time_pos
-    seg_flags = jnp.take(segment_step, seg_index)
+    seg_flags = segment_step.at[seg_index].get(mode="promise_in_bounds")
     weights = (seg_flags[None] == jnp.arange(2, dtype=jnp.int32)[:, None]).astype(jnp.float32)
     fast_disp, fast_vel, bad = run_line(
         line_count,
         time_count,
         window_scale,
         weights,
-        arrived,
+        wind_field,
         mean_wind,
         drag,
         transfer,
@@ -924,6 +964,7 @@
     )
 
     def checked():
+        arrived = lax.all_to_all(wind_field, "line", split_axis=0, concat_axis=0, tiled=True)
         return checked_loop(
             line_count,
             time_count,

time: 193 us -> 186 us (0.964)
  Pallas kernels: 156 us -> 174 us
  waiting for transfers between devices: 15.6 us -> 0 us
  starting transfers between devices: 8.59 us -> 0 us
  other arithmetic: 3.23 us -> 0.75 us
    pallas_call x1, Pallas kernels: 156 us -> 174 us  [run_line(): pl.pallas_call(body, out_shape=(row, row, jax.ShapeDtypeStruct((1, LANES)...]
    all_to_all x1 -> x0, waiting for transfers between devices: 15.6 us -> none  [local(): lax.all_to_all(wind_field, 'line', split_axis=1, concat_axis=0, tiled=True)]
    all_to_all x1 -> x0, starting transfers between devices: 8.59 us -> none  [local(): lax.all_to_all(wind_field, 'line', split_axis=1, concat_axis=0, tiled=True)]
    unnamed x21 -> x25, local copies, waits for them, and re-layouts: 5.57 us -> 6.21 us
  transfers between devices with their start and end apart: 1 -> 0, of which waited for: 1 -> 0; matrix products, arithmetic and copies ran while one was open for 1% -> 0% of each run, Pallas kernels for 0% -> 0%
where the time goes in v4:
time: 186 us
  Pallas kernels  174 us (94%)
  local copies, waits for them, and re-layouts  8.64 us (5%)
    pallas_call x1, Pallas kernels, run_line(): pl.pallas_call(body, out_shape=(row, row, jax.ShapeDtypeStruct((1, LANES)...  174 us
    unnamed x25, local copies, waits for them, and re-layouts  6.21 us

profile of v4, /device:TPU:1, one launch (start us, length us, event | category | flops | bytes accessed | tf_op | source)
XLA Modules:
  0.0 185.8 jit_solution(5690707372823641764)
XLA Ops:
  0.6 0.0 copy-start
  0.7 0.6 copy-done
  1.3 0.7 gather_fusion
  2.0 0.6 compare_convert_fusion.2.refs_0_
  2.6 3.0 %copy.186 = bf16[16,8,32,256]{3,1,2,0:T(8,128)(2,1)S(1)} copy(bf16[16,8,32,256]{3,2,1,0:T(8,128)(2,1)} %bitcast.1803) | data formatting | bytes 4194304
  5.6 0.1 cosine_convert_fusion
  5.7 0.0 copy-start.80
  5.7 0.5 convolution_convert_fusion
  6.2 0.0 copy-start.20
  6.3 0.0 copy-start.60
  6.3 0.0 copy-start.63
  6.3 0.0 copy-start.64
  6.3 0.0 copy-start.67
  6.3 0.0 copy-start.70
  6.3 0.0 copy-start.73
  6.3 0.0 copy-start.76
  6.3 0.1 copy.188
  6.5 0.0 copy-done.80
  6.5 1.6 gather_fusion.1
  8.1 0.0 copy-done.20
  8.1 0.0 copy-done.60
  8.1 0.0 copy-done.63
  8.1 0.0 copy-done.64
  8.1 0.0 copy-done.67
  8.1 0.0 copy-done.70
  8.2 0.0 copy-done.73
  8.2 0.0 copy-done.76
  8.2 174.2 %shard_map.126 = (f32[1,512]{1,0:T(1,128)}, f32[1,512]{1,0:T(1,128)}, f32[1,128]{1,0:T(1,128)}) custom-call(f32[2,32]{1,0:T(2,128)} %compare_convert_fusion.2.refs_0_, bf16[32,64,256]{2,1,0:T(8,128)(2,1)} %gather_fusion.1, f32[1,256]{1,0:T(1,128)S(1)} %copy-done.76, f32[1,256]{1,0:T(1,128)S(1)} %copy-done.67, f32[1,2,512,256]{3,2,1,0:T(8,128)S(1)} %copy-done.20, ...), custom_call_target="tpu_custom_call" | custom-call | flops 13421772800 | bytes 5242880 | tf_op jit(solution)/shard_map/pallas_call | solution.py:873
  182.9 0.3 conditional.1
  183.2 0.0 copy-start.1
  183.2 1.3 copy.281
  184.5 1.2 copy.282
  (6 shorter events, 0.0 us)
Async XLA Ops:
  0.6 0.7 copy-start
  5.7 0.7 copy-start.80
  6.2 1.9 %copy-start.20 = (f32[1,2,512,256]{3,2,1,0:T(8,128)S(1)}, f32[1,2,512,256]{3,2,1,0:T(8,128)}, u32[]{:S(2)}) copy-start(f32[1,2,512,256]{3,2,1,0:T(8,128)} %refs_4_.1) | copy-start | bytes 3145732
  6.3 1.9 %copy-start.60 = (f32[1,512,512]{2,1,0:T(8,128)S(1)}, f32[1,512,512]{2,1,0:T(8,128)}, u32[]{:S(2)}) copy-start(f32[1,512,512]{2,1,0:T(8,128)} %refs_5_.1) | copy-start | bytes 3145732
  6.3 1.9 copy-start.63
  6.3 1.8 copy-start.64
  6.3 1.8 copy-start.67
  6.3 1.8 copy-start.70
  6.3 1.8 copy-start.73
  6.3 1.8 copy-start.76
  183.2 2.5 %copy-start.1 = (s32[128]{0:T(128)S(1)}, s32[128]{0:T(128)}, u32[]{:S(2)}) copy-start(s32[128]{0:T(128)} %param.148) | copy-start | bytes 1540

commit v5 on v4

--- a/solution.py
+++ b/solution.py
@@ -233,7 +233,7 @@
     time_count,
     window_scale,
     levels,
-    weight_ref,
+    step_ref,
     sent_ref,
     mean_ref,
     drag_ref,
@@ -321,7 +321,6 @@
 
     lax.fori_loop(1, line_count, greet, 0)
     partners = partners + (line_count - 1)
-    pl.semaphore_wait(barrier, partners)
 
     def remote(source, target, sems, to_line, to_time=None):
         return pltpu.make_async_remote_copy(
@@ -446,6 +445,14 @@
     disp_ref[...] = disp_in[...]
     acc_ref[...] = acc_in[...]
     bad_ref[...] = jnp.zeros_like(bad_ref)
+    own_diag = jnp.where(eye_mask(order), accel_scale * to_column(mass_ref[...]), 0.0)
+    diag_ref[...] = span_ref[0] + own_diag
+
+    @pl.when(core == 1)
+    def _():
+        couple[0, 1] = -jnp.where(line < last, 1.0, 0.0) * span_ref[0]
+
+    pl.semaphore_wait(barrier, partners)
 
     @pl.when(core == 0)
     def _():
@@ -496,12 +503,8 @@
     lax.fori_loop(1, line_count, wind_start, 0)
     wind_ref[line] = sent_ref[line]
 
-    own_diag = jnp.where(eye_mask(order), accel_scale * to_column(mass_ref[...]), 0.0)
-    diag_ref[...] = span_ref[0] + own_diag
-
     @pl.when(core == 1)
     def _():
-        couple[0, 1] = -jnp.where(line < last, 1.0, 0.0) * span_ref[0]
         span_copy().wait_recv()
         diag_ref[...] = diag_ref[...] + prev_span[...]
         couple[0, 0] = -prev_span[...]
@@ -533,7 +536,8 @@
 
         def add(group, total):
             relative = wind_ref[group].astype(jnp.float32) + offset
-            return total + weight_ref[window, group] * (relative * jnp.abs(relative))
+            step = step_ref[group * time_count + time].astype(jnp.float32)
+            return total + (step if window == 1 else 1.0 - step) * (relative * jnp.abs(relative))
 
         total = lax.fori_loop(0, count, add, jnp.zeros((samples, width), jnp.float32))
         load = drag_ref[...] * jnp.sum(total, axis=0, keepdims=True) * window_scale
@@ -573,7 +577,7 @@
                 map_copy().wait_recv()
             side_ref[...] = side_ref[...] + to_row(mat_vec(prev_map[...], summed(1)))
 
-    def reduce_vector(window, level):
+    def send_vector(window, level):
         @pl.when(sends(level))
         def _():
             column = to_column(side_ref[...])
@@ -585,6 +589,7 @@
                 def _():
                     vec_copy(window, level, side).start()
 
+    def take_vector(window, level):
         @pl.when(core == 0)
         def _():
             for side in range(2):
@@ -597,11 +602,15 @@
                         bad_ref[...] = bad_ref[...] + vec_in[window, level, side, :, order:]
 
     def factor_level(level, carry):
+        before = jnp.maximum(level - 1, 0)
+
+        @pl.when(level == levels)
+        def _():
+            send_vector(0, before)
+
         @pl.when(sends(level))
         def _():
             newton_inverse(diag_ref, inverse_ref, bad_ref)
-
-        before = jnp.maximum(level - 1, 0)
 
         for side in range(2):
             sent = (level >= 1) & sends(before) & there(before, side)
@@ -660,7 +669,7 @@
                 for copy in update_copies(level, 1):
                     copy.start()
 
-        @pl.when(level == 0)
+        @pl.when(level == 1)
         def _():
             @pl.when(line < last)
             def _():
@@ -677,14 +686,20 @@
                 for turn in range(1, time_count):
                     share_copy(level, side, turn).start()
 
-        @pl.when(level == 0)
+        @pl.when(level == 1)
         def _():
             end_loads(0)
 
+        @pl.when((level >= 1) & (level < levels))
+        def _():
+            send_vector(0, before)
+
+        @pl.when(level >= 1)
+        def _():
+            take_vector(0, before)
+
         @pl.when(level < levels)
         def _():
-            reduce_vector(0, level)
-
             @pl.when(core == 0)
             def _():
                 for side in range(2):
@@ -789,7 +804,8 @@
     end_loads(1)
 
     def reduce_level(level, carry):
-        reduce_vector(1, level)
+        send_vector(1, level)
+        take_vector(1, level)
         return carry
 
     lax.fori_loop(0, levels, reduce_level, 0)
@@ -845,7 +861,7 @@
     line_count,
     time_count,
     window_scale,
-    weights,
+    segment_step,
     wind_field,
     mean_wind,
     drag,
@@ -915,7 +931,7 @@
         cost_estimate=pl.CostEstimate(
             flops=100 * order**3, bytes_accessed=5 * 2**20, transcendentals=0
         ),
-    )(weights, wind_field, mean_wind, drag, transfer, span_stiff, mass, disp0, vel0, acc0)
+    )(segment_step, wind_field, mean_wind, drag, transfer, span_stiff, mass, disp0, vel0, acc0)
 
 
 def local(
@@ -944,14 +960,11 @@
     wind_field = wind_field.reshape(TS, span_count, Q)
     wind_field = wind_field.at[:, span_column].get(mode="promise_in_bounds").transpose(1, 0, 2)
     window_scale = 1.0 / (TS * (seg_count // 2))
-    seg_index = jnp.arange(line_count, dtype=jnp.int32) * time_count + time_pos
-    seg_flags = segment_step.at[seg_index].get(mode="promise_in_bounds")
-    weights = (seg_flags[None] == jnp.arange(2, dtype=jnp.int32)[:, None]).astype(jnp.float32)
     fast_disp, fast_vel, bad = run_line(
         line_count,
         time_count,
         window_scale,
-        weights,
+        segment_step,
         wind_field,
         mean_wind,
         drag,
@@ -965,6 +978,8 @@
 
     def checked():
         arrived = lax.all_to_all(wind_field, "line", split_axis=0, concat_axis=0, tiled=True)
+        seg_index = jnp.arange(line_count, dtype=jnp.int32) * time_count + time_pos
+        seg_flags = jnp.take(segment_step, seg_index)
         return checked_loop(
             line_count,
             time_count,

time: 186 us -> 186 us (level)
    unnamed x25 -> x21, local copies, waits for them, and re-layouts: 6.21 us -> 5.56 us
where the time goes in v5:
time: 186 us; the launch traced here: 185 us
  Pallas kernels  174 us (94%)
  local copies, waits for them, and re-layouts  8.51 us (5%)
    pallas_call x1, Pallas kernels, run_line(): pl.pallas_call(body, out_shape=(row, row, jax.ShapeDtypeStruct((1, LANES)...  174 us
    unnamed x21, local copies, waits for them, and re-layouts  5.56 us

profile of v5, /device:TPU:1, one launch (start us, length us, event | category | flops | bytes accessed | tf_op | source)
XLA Modules:
  0.0 185.4 jit_solution(8501594573186684145)
XLA Ops:
  0.6 3.0 %copy.287 = bf16[16,8,32,256]{3,1,2,0:T(8,128)(2,1)S(1)} copy(bf16[16,8,32,256]{3,2,1,0:T(8,128)(2,1)} %bitcast.1803) | data formatting | bytes 4194304
  3.7 0.1 cosine_convert_fusion
  3.8 0.0 copy-start.76
  3.8 0.5 convolution_convert_fusion
  4.3 0.0 copy-start
  4.3 0.0 copy-start.19
  4.3 0.0 copy-start.59
  4.3 0.0 copy-start.60
  4.4 0.0 copy-start.63
  4.4 0.0 copy-start.66
  4.4 0.0 copy-start.69
  4.4 0.0 copy-start.72
  4.4 1.1 copy.289
  5.5 0.0 copy-done.76
  5.5 1.8 gather_fusion.1
  7.4 0.0 copy-done
  7.4 0.0 copy-done.19
  7.4 0.0 copy-done.59
  7.4 0.0 copy-done.60
  7.4 0.0 copy-done.63
  7.4 0.0 copy-done.66
  7.4 0.0 copy-done.69
  7.5 0.0 copy-done.72
  7.5 174.4 %shard_map.126 = (f32[1,512]{1,0:T(1,128)}, f32[1,512]{1,0:T(1,128)}, f32[1,128]{1,0:T(1,128)}) custom-call(s32[128]{0:T(128)S(1)} %copy-done, bf16[32,64,256]{2,1,0:T(8,128)(2,1)S(1)} %gather_fusion.1, f32[1,256]{1,0:T(1,128)S(1)} %copy-done.72, f32[1,256]{1,0:T(1,128)S(1)} %copy-done.63, f32[1,2,512,256]{3,2,1,0:T(8,128)S(1)} %copy-done.19, ...), custom_call_target="tpu_custom_call" | custom-call | flops 13421772800 | bytes 5242880 | tf_op jit(solution)/shard_map/pallas_call | solution.py:889
  182.6 0.3 conditional.1
  182.9 1.3 copy.382
  184.1 1.2 copy.383
  (3 shorter events, 0.0 us)
Async XLA Ops:
  3.8 1.7 copy-start.76
  4.3 3.1 %copy-start = (s32[128]{0:T(128)S(1)}, s32[128]{0:T(128)}, u32[]{:S(2)}) copy-start(s32[128]{0:T(128)} %refs_0_.1) | copy-start | bytes 1540
  4.3 3.1 %copy-start.19 = (f32[1,2,512,256]{3,2,1,0:T(8,128)S(1)}, f32[1,2,512,256]{3,2,1,0:T(8,128)}, u32[]{:S(2)}) copy-start(f32[1,2,512,256]{3,2,1,0:T(8,128)} %refs_4_.1) | copy-start | bytes 3145732
  4.3 3.1 %copy-start.59 = (f32[1,512]{1,0:T(1,128)S(1)}, f32[1,512]{1,0:T(1,128)}, u32[]{:S(2)}) copy-start(f32[1,512]{1,0:T(1,128)} %refs_8_.1) | copy-start | bytes 6148
  4.3 3.1 %copy-start.60 = (f32[1,512]{1,0:T(1,128)S(1)}, f32[1,512]{1,0:T(1,128)}, u32[]{:S(2)}) copy-start(f32[1,512]{1,0:T(1,128)} %refs_6_.1) | copy-start | bytes 6148
  4.4 3.1 %copy-start.63 = (f32[1,256]{1,0:T(1,128)S(1)}, f32[1,256]{1,0:T(1,128)}, u32[]{:S(2)}) copy-start(f32[1,256]{1,0:T(1,128)} %refs_3_.1) | copy-start | bytes 3076
  4.4 3.1 %copy-start.66 = (f32[1,512]{1,0:T(1,128)S(1)}, f32[1,512]{1,0:T(1,128)}, u32[]{:S(2)}) copy-start(f32[1,512]{1,0:T(1,128)} %refs_7_.1) | copy-start | bytes 6148
  4.4 3.1 %copy-start.69 = (f32[1,512]{1,0:T(1,128)S(1)}, f32[1,512]{1,0:T(1,128)}, u32[]{:S(2)}) copy-start(f32[1,512]{1,0:T(1,128)} %refs_9_.1) | copy-start | bytes 6148
  4.4 3.1 %copy-start.72 = (f32[1,256]{1,0:T(1,128)S(1)}, f32[1,256]{1,0:T(1,128)}, u32[]{:S(2)}) copy-start(f32[1,256]{1,0:T(1,128)} %refs_2_.1) | copy-start | bytes 3076

commit v6 on v5

--- a/solution.py
+++ b/solution.py
@@ -276,7 +276,9 @@
     load_send_sems,
     load_recv_sems,
     sol_sems,
+    halfway,
     wind_ref,
+    halfway_sems,
     wind_sems,
 ):
     line = lax.axis_index("line")
@@ -310,17 +312,40 @@
         )
     partners = partners + (time_count - 1)
 
-    def greet(turn, carry):
+    inner = max(2, line_count // 4)
+    outer = line_count // inner
+    place_x = lax.div(line, inner)
+    place_y = lax.rem(line, inner)
+    for turn in range(1, outer):
         pl.semaphore_signal(
             barrier,
             inc=1,
-            device_id=(lax.rem(line + turn, line_count), time),
+            device_id=(lax.rem(place_x + turn, outer) * inner + place_y, time),
             device_id_type=MESH,
         )
-        return carry
-
-    lax.fori_loop(1, line_count, greet, 0)
-    partners = partners + (line_count - 1)
+    for turn in range(1, inner):
+        pl.semaphore_signal(
+            barrier,
+            inc=1,
+            device_id=(place_x * inner + lax.rem(place_y + turn, inner), time),
+            device_id_type=MESH,
+        )
+    partners = partners + (outer + inner - 2)
+    stride = 1
+    while stride < inner:
+        for delta in (-stride, stride):
+            near = (line + delta >= 0) & (line + delta <= last)
+            if stride > 1:
+                near = near & (core == 0)
+
+            @pl.when(near)
+            def _():
+                pl.semaphore_signal(
+                    barrier, inc=1, device_id=(line + delta, time), device_id_type=MESH
+                )
+
+            partners = partners + jnp.where(near, 1, 0)
+        stride = stride * 2
 
     def remote(source, target, sems, to_line, to_time=None):
         return pltpu.make_async_remote_copy(
@@ -470,38 +495,45 @@
     def _():
         next_vel[...] = jnp.zeros_like(next_vel)
 
-    def wind_copy(turn):
-        to_line = lax.rem(line + turn, line_count)
+    def along_x(turn):
+        to_x = lax.rem(place_x + turn, outer)
         return remote(
-            sent_ref.at[to_line],
-            wind_ref.at[line],
-            (wind_sems.at[0, to_line], wind_sems.at[1, line]),
-            to_line,
-        )
-
-    def wind_wait(turn):
-        from_line = lax.rem(line + turn, line_count)
+            sent_ref.at[pl.ds(pl.multiple_of(to_x * inner, inner), inner)],
+            halfway.at[place_x],
+            (halfway_sems.at[0, to_x], halfway_sems.at[1, place_x]),
+            to_x * inner + place_y,
+        )
+
+    def along_x_wait(turn):
+        from_x = lax.rem(place_x + turn, outer)
         remote(
-            sent_ref.at[from_line],
-            wind_ref.at[from_line],
-            (wind_sems.at[0, from_line], wind_sems.at[1, from_line]),
-            from_line,
+            sent_ref.at[pl.ds(pl.multiple_of(from_x * inner, inner), inner)],
+            halfway.at[from_x],
+            (halfway_sems.at[0, from_x], halfway_sems.at[1, from_x]),
+            line,
         ).wait_recv()
 
-    def wind_start(turn, carry):
-        wind_copy(turn).start()
-        return carry
-
-    def wind_done(turn, carry):
-        wind_wait(turn)
-        return carry
-
-    def wind_left(turn, carry):
-        wind_copy(turn).wait_send()
-        return carry
-
-    lax.fori_loop(1, line_count, wind_start, 0)
-    wind_ref[line] = sent_ref[line]
+    def along_y(turn):
+        to_y = lax.rem(place_y + turn, inner)
+        return remote(
+            halfway.at[:, to_y],
+            wind_ref.at[:, place_y],
+            (wind_sems.at[0, to_y], wind_sems.at[1, place_y]),
+            place_x * inner + to_y,
+        )
+
+    def along_y_wait(turn):
+        from_y = lax.rem(place_y + turn, inner)
+        remote(
+            halfway.at[:, from_y],
+            wind_ref.at[:, from_y],
+            (wind_sems.at[0, from_y], wind_sems.at[1, from_y]),
+            line,
+        ).wait_recv()
+
+    for turn in range(1, outer):
+        along_x(turn).start()
+    halfway[place_x] = sent_ref[pl.ds(pl.multiple_of(place_x * inner, inner), inner)]
 
     @pl.when(core == 1)
     def _():
@@ -532,14 +564,15 @@
         next_col = to_column(next_vel[window])
         interior = vec_mat(velocity_col, maps_ref[0, 0]) + vec_mat(next_col, maps_ref[0, 1])
         offset = mean_ref[...] - interior
-        count, samples, width = wind_ref.shape
+        samples, width = wind_ref.shape[2:]
 
         def add(group, total):
-            relative = wind_ref[group].astype(jnp.float32) + offset
+            field = wind_ref[lax.div(group, inner), lax.rem(group, inner)]
+            relative = field.astype(jnp.float32) + offset
             step = step_ref[group * time_count + time].astype(jnp.float32)
             return total + (step if window == 1 else 1.0 - step) * (relative * jnp.abs(relative))
 
-        total = lax.fori_loop(0, count, add, jnp.zeros((samples, width), jnp.float32))
+        total = lax.fori_loop(0, line_count, add, jnp.zeros((samples, width), jnp.float32))
         load = drag_ref[...] * jnp.sum(total, axis=0, keepdims=True) * window_scale
         load_out[window] = load
         load_in[window, 0, time] = load
@@ -582,11 +615,11 @@
         def _():
             column = to_column(side_ref[...])
             for side in range(2):
-                vec_out[window, level, side, :, :order] = vec_mat(column, scaled[level, side])
-                vec_out[window, level, side, :, order:] = bad_ref[...]
 
                 @pl.when(there(level, side))
                 def _():
+                    vec_out[window, level, side, :, :order] = vec_mat(column, scaled[level, side])
+                    vec_out[window, level, side, :, order:] = bad_ref[...]
                     vec_copy(window, level, side).start()
 
     def take_vector(window, level):
@@ -601,6 +634,22 @@
                     if window == 1:
                         bad_ref[...] = bad_ref[...] + vec_in[window, level, side, :, order:]
 
+    def loads_left(window):
+        for turn in range(1, time_count):
+            load_copy(window, turn).wait_send()
+
+        @pl.when(line < last)
+        def _():
+            for turn in range(time_count, 2 * time_count):
+                load_copy(window, turn).wait_send()
+
+    def vectors_left(window, level):
+        for side in range(2):
+
+            @pl.when(sends(level) & there(level, side))
+            def _():
+                vec_copy(window, level, side).wait_send()
+
     def factor_level(level, carry):
         before = jnp.maximum(level - 1, 0)
 
@@ -640,43 +689,58 @@
         @pl.when(sends(level) & (level < levels))
         def _():
             coupling(0)
-            scaled[level, 0] = split_dot(inverse_ref[...], couple[level, 0], 1, 1)
+
+            @pl.when(there(level, 0))
+            def _():
+                scaled[level, 0] = split_dot(inverse_ref[...], couple[level, 0], 1, 1)
+
             coupling(1)
-            scaled[level, 1] = split_dot(inverse_ref[...], couple[level, 1])
+
+            @pl.when(there(level, 1))
+            def _():
+                scaled[level, 1] = split_dot(inverse_ref[...], couple[level, 1])
 
             @pl.when(level < levels - 1)
             def _():
                 rows = pl.ds(pl.multiple_of(time * quarter, quarter), quarter)
-                couple_out[...] = -split_dot(couple[level, 0, rows], scaled[level, 1])
+                both = there(level, 0) & there(level, 1)
+
+                @pl.when(both)
+                def _():
+                    couple_out[...] = -split_dot(couple[level, 0, rows], scaled[level, 1])
+
+                @pl.when(jnp.logical_not(both))
+                def _():
+                    couple_out[...] = jnp.zeros_like(couple_out)
+
                 for side in range(2):
 
                     @pl.when(there(level, side))
                     def _():
                         couple_copy(level, side).start()
 
-            update_out[0] = split_dot(couple[level, 0], scaled[level, 0])
-
             @pl.when(there(level, 0))
             def _():
+                update_out[0] = split_dot(couple[level, 0], scaled[level, 0])
                 for copy in update_copies(level, 0):
                     copy.start()
 
-            own = jnp.where(level == 0, 1.0, 0.0)
-            update_out[1] = split_dot(couple[level, 1], scaled[level, 1], 0, 0) - own * span_ref[0]
-
             @pl.when(there(level, 1))
             def _():
+                own = jnp.where(level == 0, 1.0, 0.0)
+                update_out[1] = (
+                    split_dot(couple[level, 1], scaled[level, 1], 0, 0) - own * span_ref[0]
+                )
                 for copy in update_copies(level, 1):
                     copy.start()
 
-        @pl.when(level == 1)
-        def _():
-            @pl.when(line < last)
-            def _():
-                vel_wait(0)
-
-            lax.fori_loop(1, line_count, wind_done, 0)
-            begin_loads(0)
+        @pl.when(level == 0)
+        def _():
+            for turn in range(1, outer):
+                along_x_wait(turn)
+            for turn in range(1, inner):
+                along_y(turn).start()
+            wind_ref[:, place_y] = halfway[:, place_y]
 
         for side in range(2):
 
@@ -688,7 +752,34 @@
 
         @pl.when(level == 1)
         def _():
+            @pl.when(line < last)
+            def _():
+                vel_wait(0)
+
+            for turn in range(1, inner):
+                along_y_wait(turn)
+            begin_loads(0)
             end_loads(0)
+
+        @pl.when(level == 2)
+        def _():
+            for turn in range(1, outer):
+                along_x(turn).wait_send()
+            for turn in range(1, inner):
+                along_y(turn).wait_send()
+            loads_left(0)
+
+            @pl.when(core == 0)
+            def _():
+                span_copy().wait_send()
+
+            @pl.when(line < last)
+            def _():
+                map_copy().wait_send()
+
+        @pl.when(level >= 2)
+        def _():
+            vectors_left(0, level - 2)
 
         @pl.when((level >= 1) & (level < levels))
         def _():
@@ -817,24 +908,9 @@
     finish(1)
     bad_out[...] = bad_ref[...]
 
-    lax.fori_loop(1, line_count, wind_left, 0)
-
-    @pl.when(core == 0)
-    def _():
-        span_copy().wait_send()
-
-    @pl.when(line < last)
-    def _():
-        map_copy().wait_send()
+    loads_left(1)
 
     for window in range(2):
-        for turn in range(1, time_count):
-            load_copy(window, turn).wait_send()
-
-        @pl.when(line < last)
-        def _():
-            for turn in range(time_count, 2 * time_count):
-                load_copy(window, turn).wait_send()
 
         @pl.when(core == 0)
         def _():
@@ -844,14 +920,10 @@
             def _():
                 sol_copy(window, 0).wait_send()
 
+    vectors_left(0, levels - 1)
+
     def drain(level, carry):
-        for window in range(2):
-            for side in range(2):
-
-                @pl.when(sends(level) & there(level, side))
-                def _():
-                    vec_copy(window, level, side).wait_send()
-
+        vectors_left(1, level)
         return carry
 
     lax.fori_loop(0, levels, drain, 0)
@@ -876,6 +948,8 @@
     width = mean_wind.shape[-1]
     levels = (line_count - 1).bit_length()
     row = jax.ShapeDtypeStruct((1, order), jnp.float32)
+    inner = max(2, line_count // 4)
+    outer = line_count // inner
 
     def body(*refs):
         line_kernel(line_count, time_count, window_scale, levels, *refs)
@@ -922,8 +996,10 @@
             dma((2, 2 * time_count)),
             dma((2, 2, time_count)),
             dma((2, 2, 2)),
-            pltpu.VMEM(wind_field.shape, wind_field.dtype),
-            dma((2, line_count)),
+            pltpu.VMEM((outer, inner) + wind_field.shape[1:], wind_field.dtype),
+            pltpu.VMEM((outer, inner) + wind_field.shape[1:], wind_field.dtype),
+            dma((2, outer)),
+            dma((2, inner)),
         ],
         compiler_params=pltpu.CompilerParams(
             collective_id=0, has_side_effects=True, vmem_limit_bytes=60 * 2**20

time: 186 us -> 187 us (level)
  Pallas kernels: 174 us -> 176 us
where the time goes in v6:
time: 187 us
  Pallas kernels  176 us (94%)
  local copies, waits for them, and re-layouts  8.51 us (5%)
    pallas_call x1, Pallas kernels, run_line(): pl.pallas_call(body, out_shape=(row, row, jax.ShapeDtypeStruct((1, LANES)...  176 us
    unnamed x21, local copies, waits for them, and re-layouts  5.56 us

profile of v6, /device:TPU:1, one launch (start us, length us, event | category | flops | bytes accessed | tf_op | source)
XLA Modules:
  0.0 187.0 jit_solution(15971357370509530599)
XLA Ops:
  0.6 3.0 %copy.287 = bf16[16,8,32,256]{3,1,2,0:T(8,128)(2,1)S(1)} copy(bf16[16,8,32,256]{3,2,1,0:T(8,128)(2,1)} %bitcast.1803) | data formatting | bytes 4194304
  3.7 0.1 cosine_convert_fusion
  3.8 0.0 copy-start.76
  3.8 0.5 convolution_convert_fusion
  4.3 0.0 copy-start
  4.3 0.0 copy-start.19
  4.3 0.0 copy-start.59
  4.3 0.0 copy-start.60
  4.4 0.0 copy-start.63
  4.4 0.0 copy-start.66
  4.4 0.0 copy-start.69
  4.4 0.0 copy-start.72
  4.4 1.1 copy.289
  5.5 0.0 copy-done.76
  5.5 1.8 gather_fusion.1
  7.4 0.0 copy-done
  7.4 0.0 copy-done.19
  7.4 0.0 copy-done.59
  7.4 0.0 copy-done.60
  7.4 0.0 copy-done.63
  7.4 0.0 copy-done.66
  7.4 0.0 copy-done.69
  7.5 0.0 copy-done.72
  7.5 176.0 %shard_map.126 = (f32[1,512]{1,0:T(1,128)}, f32[1,512]{1,0:T(1,128)}, f32[1,128]{1,0:T(1,128)}) custom-call(s32[128]{0:T(128)S(1)} %copy-done, bf16[32,64,256]{2,1,0:T(8,128)(2,1)S(1)} %gather_fusion.1, f32[1,256]{1,0:T(1,128)S(1)} %copy-done.72, f32[1,256]{1,0:T(1,128)S(1)} %copy-done.63, f32[1,2,512,256]{3,2,1,0:T(8,128)S(1)} %copy-done.19, ...), custom_call_target="tpu_custom_call" | custom-call | flops 13421772800 | bytes 5242880 | tf_op jit(solution)/shard_map/pallas_call | solution.py:963
  184.2 0.3 conditional.1
  184.5 1.3 copy.382
  185.7 1.2 copy.383
  (3 shorter events, 0.0 us)
Async XLA Ops:
  3.8 1.7 copy-start.76
  4.3 3.1 %copy-start = (s32[128]{0:T(128)S(1)}, s32[128]{0:T(128)}, u32[]{:S(2)}) copy-start(s32[128]{0:T(128)} %refs_0_.1) | copy-start | bytes 1540
  4.3 3.1 %copy-start.19 = (f32[1,2,512,256]{3,2,1,0:T(8,128)S(1)}, f32[1,2,512,256]{3,2,1,0:T(8,128)}, u32[]{:S(2)}) copy-start(f32[1,2,512,256]{3,2,1,0:T(8,128)} %refs_4_.1) | copy-start | bytes 3145732
  4.3 3.1 %copy-start.59 = (f32[1,512]{1,0:T(1,128)S(1)}, f32[1,512]{1,0:T(1,128)}, u32[]{:S(2)}) copy-start(f32[1,512]{1,0:T(1,128)} %refs_8_.1) | copy-start | bytes 6148
  4.3 3.1 %copy-start.60 = (f32[1,512]{1,0:T(1,128)S(1)}, f32[1,512]{1,0:T(1,128)}, u32[]{:S(2)}) copy-start(f32[1,512]{1,0:T(1,128)} %refs_6_.1) | copy-start | bytes 6148
  4.4 3.1 %copy-start.63 = (f32[1,256]{1,0:T(1,128)S(1)}, f32[1,256]{1,0:T(1,128)}, u32[]{:S(2)}) copy-start(f32[1,256]{1,0:T(1,128)} %refs_3_.1) | copy-start | bytes 3076
  4.4 3.1 %copy-start.66 = (f32[1,512]{1,0:T(1,128)S(1)}, f32[1,512]{1,0:T(1,128)}, u32[]{:S(2)}) copy-start(f32[1,512]{1,0:T(1,128)} %refs_7_.1) | copy-start | bytes 6148
  4.4 3.1 %copy-start.69 = (f32[1,512]{1,0:T(1,128)S(1)}, f32[1,512]{1,0:T(1,128)}, u32[]{:S(2)}) copy-start(f32[1,512]{1,0:T(1,128)} %refs_9_.1) | copy-start | bytes 6148
  4.4 3.1 %copy-start.72 = (f32[1,256]{1,0:T(1,128)S(1)}, f32[1,256]{1,0:T(1,128)}, u32[]{:S(2)}) copy-start(f32[1,256]{1,0:T(1,128)} %refs_2_.1) | copy-start | bytes 3076

commit v7 on v6

--- a/solution.py
+++ b/solution.py
@@ -495,45 +495,45 @@
     def _():
         next_vel[...] = jnp.zeros_like(next_vel)
 
+    def along_y(turn):
+        to_y = lax.rem(place_y + turn, inner)
+        return remote(
+            sent_ref.at[:, to_y],
+            halfway.at[:, place_y],
+            (halfway_sems.at[0, to_y], halfway_sems.at[1, place_y]),
+            place_x * inner + to_y,
+        )
+
+    def along_y_wait(turn):
+        from_y = lax.rem(place_y + turn, inner)
+        remote(
+            sent_ref.at[:, from_y],
+            halfway.at[:, from_y],
+            (halfway_sems.at[0, from_y], halfway_sems.at[1, from_y]),
+            line,
+        ).wait_recv()
+
     def along_x(turn):
         to_x = lax.rem(place_x + turn, outer)
         return remote(
-            sent_ref.at[pl.ds(pl.multiple_of(to_x * inner, inner), inner)],
-            halfway.at[place_x],
-            (halfway_sems.at[0, to_x], halfway_sems.at[1, place_x]),
+            halfway.at[to_x],
+            wind_ref.at[place_x],
+            (wind_sems.at[0, to_x], wind_sems.at[1, place_x]),
             to_x * inner + place_y,
         )
 
     def along_x_wait(turn):
         from_x = lax.rem(place_x + turn, outer)
         remote(
-            sent_ref.at[pl.ds(pl.multiple_of(from_x * inner, inner), inner)],
             halfway.at[from_x],
-            (halfway_sems.at[0, from_x], halfway_sems.at[1, from_x]),
+            wind_ref.at[from_x],
+            (wind_sems.at[0, from_x], wind_sems.at[1, from_x]),
             line,
         ).wait_recv()
 
-    def along_y(turn):
-        to_y = lax.rem(place_y + turn, inner)
-        return remote(
-            halfway.at[:, to_y],
-            wind_ref.at[:, place_y],
-            (wind_sems.at[0, to_y], wind_sems.at[1, place_y]),
-            place_x * inner + to_y,
-        )
-
-    def along_y_wait(turn):
-        from_y = lax.rem(place_y + turn, inner)
-        remote(
-            halfway.at[:, from_y],
-            wind_ref.at[:, from_y],
-            (wind_sems.at[0, from_y], wind_sems.at[1, from_y]),
-            line,
-        ).wait_recv()
-
-    for turn in range(1, outer):
-        along_x(turn).start()
-    halfway[place_x] = sent_ref[pl.ds(pl.multiple_of(place_x * inner, inner), inner)]
+    for turn in range(1, inner):
+        along_y(turn).start()
+    halfway[:, place_y] = sent_ref[:, place_y]
 
     @pl.when(core == 1)
     def _():
@@ -734,14 +734,6 @@
                 for copy in update_copies(level, 1):
                     copy.start()
 
-        @pl.when(level == 0)
-        def _():
-            for turn in range(1, outer):
-                along_x_wait(turn)
-            for turn in range(1, inner):
-                along_y(turn).start()
-            wind_ref[:, place_y] = halfway[:, place_y]
-
         for side in range(2):
 
             @pl.when((level < levels - 1) & (core == 0) & there(level, side))
@@ -750,19 +742,42 @@
                 for turn in range(1, time_count):
                     share_copy(level, side, turn).start()
 
-        @pl.when(level == 1)
-        def _():
-            @pl.when(line < last)
-            def _():
-                vel_wait(0)
-
+        @pl.when(level == 0)
+        def _():
             for turn in range(1, inner):
                 along_y_wait(turn)
+            for turn in range(1, outer):
+                along_x(turn).start()
+            wind_ref[place_x] = halfway[place_x]
+
+        @pl.when(level == 1)
+        def _():
+            @pl.when(line < last)
+            def _():
+                vel_wait(0)
+
+            for turn in range(1, outer):
+                along_x_wait(turn)
             begin_loads(0)
+
+        @pl.when(level == 2)
+        def _():
             end_loads(0)
-
-        @pl.when(level == 2)
-        def _():
+            send_vector(0, level - 2)
+            take_vector(0, level - 2)
+
+        @pl.when((level >= 2) & (level < levels))
+        def _():
+            send_vector(0, before)
+
+        @pl.when(level >= 2)
+        def _():
+            take_vector(0, before)
+            vectors_left(0, before)
+
+        @pl.when(level == 3)
+        def _():
+            vectors_left(0, level - 3)
             for turn in range(1, outer):
                 along_x(turn).wait_send()
             for turn in range(1, inner):
@@ -776,18 +791,6 @@
             @pl.when(line < last)
             def _():
                 map_copy().wait_send()
-
-        @pl.when(level >= 2)
-        def _():
-            vectors_left(0, level - 2)
-
-        @pl.when((level >= 1) & (level < levels))
-        def _():
-            send_vector(0, before)
-
-        @pl.when(level >= 1)
-        def _():
-            take_vector(0, before)
 
         @pl.when(level < levels)
         def _():
@@ -919,8 +922,6 @@
             @pl.when(line > 0)
             def _():
                 sol_copy(window, 0).wait_send()
-
-    vectors_left(0, levels - 1)
 
     def drain(level, carry):
         vectors_left(1, level)
@@ -950,6 +951,7 @@
     row = jax.ShapeDtypeStruct((1, order), jnp.float32)
     inner = max(2, line_count // 4)
     outer = line_count // inner
+    wind_field = wind_field.reshape((outer, inner) + wind_field.shape[1:])
 
     def body(*refs):
         line_kernel(line_count, time_count, window_scale, levels, *refs)
@@ -996,10 +998,10 @@
             dma((2, 2 * time_count)),
             dma((2, 2, time_count)),
             dma((2, 2, 2)),
-            pltpu.VMEM((outer, inner) + wind_field.shape[1:], wind_field.dtype),
-            pltpu.VMEM((outer, inner) + wind_field.shape[1:], wind_field.dtype),
+            pltpu.VMEM(wind_field.shape, wind_field.dtype),
+            pltpu.VMEM(wind_field.shape, wind_field.dtype),
+            dma((2, inner)),
             dma((2, outer)),
-            dma((2, inner)),
         ],
         compiler_params=pltpu.CompilerParams(
             collective_id=0, has_side_effects=True, vmem_limit_bytes=60 * 2**20

time: 187 us -> 181 us (0.968)
  Pallas kernels: 176 us -> 170 us
    pallas_call x1, Pallas kernels: 176 us -> 170 us  [run_line(): pl.pallas_call(body, out_shape=(row, row, jax.ShapeDtypeStruct((1, LANES)...]
where the time goes in v7:
time: 181 us
  Pallas kernels  170 us (94%)
  local copies, waits for them, and re-layouts  8.51 us (5%)
    pallas_call x1, Pallas kernels, run_line(): pl.pallas_call(body, out_shape=(row, row, jax.ShapeDtypeStruct((1, LANES)...  170 us
    unnamed x21, local copies, waits for them, and re-layouts  5.56 us

profile of v7, /device:TPU:1, one launch (start us, length us, event | category | flops | bytes accessed | tf_op | source)
XLA Modules:
  0.0 180.5 jit_solution(5136803158279022569)
XLA Ops:
  0.6 3.0 %copy.287 = bf16[16,8,32,256]{3,1,2,0:T(8,128)(2,1)S(1)} copy(bf16[16,8,32,256]{3,2,1,0:T(8,128)(2,1)} %bitcast.1805) | data formatting | bytes 4194304
  3.7 0.1 cosine_convert_fusion
  3.8 0.0 copy-start.76
  3.8 0.5 convolution_convert_fusion
  4.3 0.0 copy-start
  4.3 0.0 copy-start.19
  4.3 0.0 copy-start.59
  4.3 0.0 copy-start.60
  4.4 0.0 copy-start.63
  4.4 0.0 copy-start.66
  4.4 0.0 copy-start.69
  4.4 0.0 copy-start.72
  4.4 1.1 copy.289
  5.5 0.0 copy-done.76
  5.5 1.8 %gather_fusion.1 = bf16[32,64,256]{2,1,0:T(8,128)(2,1)S(1)} fusion(bf16[64,32,256]{2,0,1:T(8,128)(2,1)} %bitcast.1804, s32[1024]{0:T(1024)S(1)} %pad_clamp_fusion.1), kind=kCustom, calls=%fused_computation.1 | custom fusion | bytes 2097280 | tf_op jit(solution)/shard_map/gather | solution.py:1039
  7.4 0.0 copy-done
  7.4 0.0 copy-done.19
  7.4 0.0 copy-done.59
  7.4 0.0 copy-done.60
  7.4 0.0 copy-done.63
  7.4 0.0 copy-done.66
  7.4 0.0 copy-done.69
  7.5 0.0 copy-done.72
  7.5 169.6 %shard_map.126 = (f32[1,512]{1,0:T(1,128)}, f32[1,512]{1,0:T(1,128)}, f32[1,128]{1,0:T(1,128)}) custom-call(s32[128]{0:T(128)S(1)} %copy-done, bf16[4,8,64,256]{3,2,1,0:T(8,128)(2,1)S(1)} %bitcast.1803, f32[1,256]{1,0:T(1,128)S(1)} %copy-done.72, f32[1,256]{1,0:T(1,128)S(1)} %copy-done.63, f32[1,2,512,256]{3,2,1,0:T(8,128)S(1)} %copy-done.19, ...), custom_call_target="tpu_custom_call" | custom-call | flops 13421772800 | bytes 5242880 | tf_op jit(solution)/shard_map/pallas_call | solution.py:965
  177.8 0.3 conditional.1
  178.0 1.3 copy.382
  179.3 1.2 copy.383
  (3 shorter events, 0.0 us)
Async XLA Ops:
  3.8 1.7 copy-start.76
  4.3 3.1 %copy-start = (s32[128]{0:T(128)S(1)}, s32[128]{0:T(128)}, u32[]{:S(2)}) copy-start(s32[128]{0:T(128)} %refs_0_.1) | copy-start | bytes 1540
  4.3 3.1 %copy-start.19 = (f32[1,2,512,256]{3,2,1,0:T(8,128)S(1)}, f32[1,2,512,256]{3,2,1,0:T(8,128)}, u32[]{:S(2)}) copy-start(f32[1,2,512,256]{3,2,1,0:T(8,128)} %refs_4_.1) | copy-start | bytes 3145732
  4.3 3.1 %copy-start.59 = (f32[1,512]{1,0:T(1,128)S(1)}, f32[1,512]{1,0:T(1,128)}, u32[]{:S(2)}) copy-start(f32[1,512]{1,0:T(1,128)} %refs_8_.1) | copy-start | bytes 6148
  4.3 3.1 %copy-start.60 = (f32[1,512]{1,0:T(1,128)S(1)}, f32[1,512]{1,0:T(1,128)}, u32[]{:S(2)}) copy-start(f32[1,512]{1,0:T(1,128)} %refs_6_.1) | copy-start | bytes 6148
  4.4 3.1 %copy-start.63 = (f32[1,256]{1,0:T(1,128)S(1)}, f32[1,256]{1,0:T(1,128)}, u32[]{:S(2)}) copy-start(f32[1,256]{1,0:T(1,128)} %refs_3_.1) | copy-start | bytes 3076
  4.4 3.1 %copy-start.66 = (f32[1,512]{1,0:T(1,128)S(1)}, f32[1,512]{1,0:T(1,128)}, u32[]{:S(2)}) copy-start(f32[1,512]{1,0:T(1,128)} %refs_7_.1) | copy-start | bytes 6148
  4.4 3.1 %copy-start.69 = (f32[1,512]{1,0:T(1,128)S(1)}, f32[1,512]{1,0:T(1,128)}, u32[]{:S(2)}) copy-start(f32[1,512]{1,0:T(1,128)} %refs_9_.1) | copy-start | bytes 6148
  4.4 3.1 %copy-start.72 = (f32[1,256]{1,0:T(1,128)S(1)}, f32[1,256]{1,0:T(1,128)}, u32[]{:S(2)}) copy-start(f32[1,256]{1,0:T(1,128)} %refs_2_.1) | copy-start | bytes 3076

commit v8 on v7

--- a/solution.py
+++ b/solution.py
@@ -566,13 +566,17 @@
         offset = mean_ref[...] - interior
         samples, width = wind_ref.shape[2:]
 
-        def add(group, total):
-            field = wind_ref[lax.div(group, inner), lax.rem(group, inner)]
-            relative = field.astype(jnp.float32) + offset
-            step = step_ref[group * time_count + time].astype(jnp.float32)
-            return total + (step if window == 1 else 1.0 - step) * (relative * jnp.abs(relative))
-
-        total = lax.fori_loop(0, line_count, add, jnp.zeros((samples, width), jnp.float32))
+        def add(from_y, total):
+            for from_x in range(outer):
+                relative = wind_ref[from_x, from_y].astype(jnp.float32) + offset
+                group = (from_x * inner + from_y) * time_count + time
+                step = step_ref[group].astype(jnp.float32)
+                total = total + (step if window == 1 else 1.0 - step) * (
+                    relative * jnp.abs(relative)
+                )
+            return total
+
+        total = lax.fori_loop(0, inner, add, jnp.zeros((samples, width), jnp.float32))
         load = drag_ref[...] * jnp.sum(total, axis=0, keepdims=True) * window_scale
         load_out[window] = load
         load_in[window, 0, time] = load
@@ -694,6 +698,19 @@
             def _():
                 scaled[level, 0] = split_dot(inverse_ref[...], couple[level, 0], 1, 1)
 
+            half = order // 2
+
+            @pl.when(there(level, 0))
+            def _():
+                copies = update_copies(level, 0)
+                for start in (0, half):
+                    rows, columns = pl.ds(start, half), pl.ds(start, order - start)
+                    update_out[0, rows, columns] = split_dot(
+                        couple[level, 0, rows], scaled[level, 0, :, columns]
+                    )
+                    for block in range(start // LANES, (start + half) // LANES):
+                        copies[block].start()
+
             coupling(1)
 
             @pl.when(there(level, 1))
@@ -719,20 +736,18 @@
                     def _():
                         couple_copy(level, side).start()
 
-            @pl.when(there(level, 0))
-            def _():
-                update_out[0] = split_dot(couple[level, 0], scaled[level, 0])
-                for copy in update_copies(level, 0):
-                    copy.start()
-
             @pl.when(there(level, 1))
             def _():
                 own = jnp.where(level == 0, 1.0, 0.0)
-                update_out[1] = (
-                    split_dot(couple[level, 1], scaled[level, 1], 0, 0) - own * span_ref[0]
-                )
-                for copy in update_copies(level, 1):
-                    copy.start()
+                copies = update_copies(level, 1)
+                for start in (0, half):
+                    rows, columns = pl.ds(start, half), pl.ds(start, order - start)
+                    update_out[1, rows, columns] = (
+                        split_dot(couple[level, 1, :, rows], scaled[level, 1, :, columns], 0, 0)
+                        - own * span_ref[0, rows, columns]
+                    )
+                    for block in range(start // LANES, (start + half) // LANES):
+                        copies[block].start()
 
         for side in range(2):
 
@@ -1074,7 +1089,13 @@
             window_scale,
         )
 
-    return lax.cond(bad[0, 0] < 0.5, lambda: (fast_disp, fast_vel), checked)
+    def chosen():
+        return jnp.concatenate(checked(), axis=0)
+
+    both = lax.cond(
+        bad[0, 0] < 0.5, lambda: jnp.concatenate([fast_disp, fast_vel], axis=0), chosen
+    )
+    return both[:1], both[1:]
 
 
 def solution(mesh):

time: 181 us -> 178 us (0.983)
  Pallas kernels: 170 us -> 168 us
  local copies, waits for them, and re-layouts: 8.51 us -> 6.61 us
    unnamed x21 -> x19, local copies, waits for them, and re-layouts: 5.56 us -> 3.07 us
where the time goes in v8:
time: 178 us
  Pallas kernels  168 us (94%)
  local copies, waits for them, and re-layouts  6.61 us (4%)
    pallas_call x1, Pallas kernels, run_line(): pl.pallas_call(body, out_shape=(row, row, jax.ShapeDtypeStruct((1, LANES)...  168 us

profile of v8, /device:TPU:1, one launch (start us, length us, event | category | flops | bytes accessed | tf_op | source)
XLA Modules:
  0.0 178.1 jit_solution(18102032914142746881)
XLA Ops:
  0.6 3.0 %copy.283 = bf16[16,8,32,256]{3,1,2,0:T(8,128)(2,1)S(1)} copy(bf16[16,8,32,256]{3,2,1,0:T(8,128)(2,1)} %bitcast.1805) | data formatting | bytes 4194304
  3.7 0.1 cosine_convert_fusion
  3.8 0.0 copy-start.76
  3.8 0.5 convolution_convert_fusion
  4.3 0.0 copy-start
  4.3 0.0 copy-start.19
  4.3 0.0 copy-start.59
  4.3 0.0 copy-start.60
  4.4 0.0 copy-start.63
  4.4 0.0 copy-start.66
  4.4 0.0 copy-start.69
  4.4 0.0 copy-start.72
  4.4 1.1 copy.285
  5.5 0.0 copy-done.76
  5.5 1.8 %gather_fusion.1 = bf16[32,64,256]{2,1,0:T(8,128)(2,1)S(1)} fusion(bf16[64,32,256]{2,0,1:T(8,128)(2,1)} %bitcast.1804, s32[1024]{0:T(1024)S(1)} %pad_clamp_fusion.1), kind=kCustom, calls=%fused_computation.1 | custom fusion | bytes 2097280 | tf_op jit(solution)/shard_map/gather | solution.py:1054
  7.4 0.0 copy-done
  7.4 0.0 copy-done.19
  7.4 0.0 copy-done.59
  7.4 0.0 copy-done.60
  7.4 0.0 copy-done.63
  7.4 0.0 copy-done.66
  7.4 0.0 copy-done.69
  7.5 0.0 copy-done.72
  7.5 168.4 %shard_map.122 = (f32[1,512]{1,0:T(1,128)}, f32[1,512]{1,0:T(1,128)}, f32[1,128]{1,0:T(1,128)}) custom-call(s32[128]{0:T(128)S(1)} %copy-done, bf16[4,8,64,256]{3,2,1,0:T(8,128)(2,1)S(1)} %bitcast.1803, f32[1,256]{1,0:T(1,128)S(1)} %copy-done.72, f32[1,256]{1,0:T(1,128)S(1)} %copy-done.63, f32[1,2,512,256]{3,2,1,0:T(8,128)S(1)} %copy-done.19, ...), custom_call_target="tpu_custom_call" | custom-call | flops 13421772800 | bytes 5242880 | tf_op jit(solution)/shard_map/pallas_call | solution.py:980
  176.5 1.0 conditional.1
  176.8 0.7 pad_maximum_fusion
  177.5 0.6 fusion.1129
  (3 shorter events, 0.0 us)
Async XLA Ops:
  3.8 1.7 copy-start.76
  4.3 3.1 %copy-start = (s32[128]{0:T(128)S(1)}, s32[128]{0:T(128)}, u32[]{:S(2)}) copy-start(s32[128]{0:T(128)} %refs_0_.1) | copy-start | bytes 1540
  4.3 3.1 %copy-start.19 = (f32[1,2,512,256]{3,2,1,0:T(8,128)S(1)}, f32[1,2,512,256]{3,2,1,0:T(8,128)}, u32[]{:S(2)}) copy-start(f32[1,2,512,256]{3,2,1,0:T(8,128)} %refs_4_.1) | copy-start | bytes 3145732
  4.3 3.1 %copy-start.59 = (f32[1,512]{1,0:T(1,128)S(1)}, f32[1,512]{1,0:T(1,128)}, u32[]{:S(2)}) copy-start(f32[1,512]{1,0:T(1,128)} %refs_8_.1) | copy-start | bytes 6148
  4.3 3.1 %copy-start.60 = (f32[1,512]{1,0:T(1,128)S(1)}, f32[1,512]{1,0:T(1,128)}, u32[]{:S(2)}) copy-start(f32[1,512]{1,0:T(1,128)} %refs_6_.1) | copy-start | bytes 6148
  4.4 3.1 %copy-start.63 = (f32[1,256]{1,0:T(1,128)S(1)}, f32[1,256]{1,0:T(1,128)}, u32[]{:S(2)}) copy-start(f32[1,256]{1,0:T(1,128)} %refs_3_.1) | copy-start | bytes 3076
  4.4 3.1 %copy-start.66 = (f32[1,512]{1,0:T(1,128)S(1)}, f32[1,512]{1,0:T(1,128)}, u32[]{:S(2)}) copy-start(f32[1,512]{1,0:T(1,128)} %refs_7_.1) | copy-start | bytes 6148
  4.4 3.1 %copy-start.69 = (f32[1,512]{1,0:T(1,128)S(1)}, f32[1,512]{1,0:T(1,128)}, u32[]{:S(2)}) copy-start(f32[1,512]{1,0:T(1,128)} %refs_9_.1) | copy-start | bytes 6148
  4.4 3.1 %copy-start.72 = (f32[1,256]{1,0:T(1,128)S(1)}, f32[1,256]{1,0:T(1,128)}, u32[]{:S(2)}) copy-start(f32[1,256]{1,0:T(1,128)} %refs_2_.1) | copy-start | bytes 3076

commit v9 on v8

--- a/solution.py
+++ b/solution.py
@@ -561,9 +561,17 @@
 
     def begin_loads(window):
         velocity_col = to_column(vel_ref[...])
+        own_offset = mean_ref[...] - vec_mat(velocity_col, maps_ref[0, 0])
+        side_ref[...] = mass_ref[...] * (
+            accel_scale * disp_ref[...] + velocity_scale * vel_ref[...] + acc_ref[...]
+        )
+
+        @pl.when((line < last) if window == 0 else (core == 0))
+        def _():
+            vel_wait(window)
+
         next_col = to_column(next_vel[window])
-        interior = vec_mat(velocity_col, maps_ref[0, 0]) + vec_mat(next_col, maps_ref[0, 1])
-        offset = mean_ref[...] - interior
+        offset = own_offset - vec_mat(next_col, maps_ref[0, 1])
         samples, width = wind_ref.shape[2:]
 
         def add(from_y, total):
@@ -603,10 +611,7 @@
                 total = total + load_in[window, step, group]
             return total
 
-        inertia = mass_ref[...] * (
-            accel_scale * disp_ref[...] + velocity_scale * vel_ref[...] + acc_ref[...]
-        )
-        side_ref[...] = inertia + to_row(mat_vec(maps_ref[0, 0], summed(0)))
+        side_ref[...] = side_ref[...] + to_row(mat_vec(maps_ref[0, 0], summed(0)))
 
         @pl.when(line > 0)
         def _():
@@ -767,10 +772,6 @@
 
         @pl.when(level == 1)
         def _():
-            @pl.when(line < last)
-            def _():
-                vel_wait(0)
-
             for turn in range(1, outer):
                 along_x_wait(turn)
             begin_loads(0)
@@ -904,10 +905,6 @@
                 vel_copy(1).start()
 
     finish(0)
-
-    @pl.when(core == 0)
-    def _():
-        vel_wait(1)
 
     begin_loads(1)
     end_loads(1)

time: 178 us -> 178 us (level)
  no operation moved by 1% of the time
where the time goes in v9:
time: 178 us
  Pallas kernels  168 us (94%)
  local copies, waits for them, and re-layouts  6.61 us (4%)
    pallas_call x1, Pallas kernels, run_line(): pl.pallas_call(body, out_shape=(row, row, jax.ShapeDtypeStruct((1, LANES)...  168 us

profile of v9, /device:TPU:1, one launch (start us, length us, event | category | flops | bytes accessed | tf_op | source)
XLA Modules:
  0.0 178.1 jit_solution(711443211394132563)
XLA Ops:
  0.6 3.0 %copy.283 = bf16[16,8,32,256]{3,1,2,0:T(8,128)(2,1)S(1)} copy(bf16[16,8,32,256]{3,2,1,0:T(8,128)(2,1)} %bitcast.1805) | data formatting | bytes 4194304
  3.7 0.1 cosine_convert_fusion
  3.8 0.0 copy-start.76
  3.8 0.5 convolution_convert_fusion
  4.3 0.0 copy-start
  4.3 0.0 copy-start.19
  4.3 0.0 copy-start.59
  4.3 0.0 copy-start.60
  4.4 0.0 copy-start.63
  4.4 0.0 copy-start.66
  4.4 0.0 copy-start.69
  4.4 0.0 copy-start.72
  4.4 1.1 copy.285
  5.5 0.0 copy-done.76
  5.5 1.8 %gather_fusion.1 = bf16[32,64,256]{2,1,0:T(8,128)(2,1)S(1)} fusion(bf16[64,32,256]{2,0,1:T(8,128)(2,1)} %bitcast.1804, s32[1024]{0:T(1024)S(1)} %pad_clamp_fusion.1), kind=kCustom, calls=%fused_computation.1 | custom fusion | bytes 2097280 | tf_op jit(solution)/shard_map/gather | solution.py:1051
  7.4 0.0 copy-done
  7.4 0.0 copy-done.19
  7.4 0.0 copy-done.59
  7.4 0.0 copy-done.60
  7.4 0.0 copy-done.63
  7.4 0.0 copy-done.66
  7.4 0.0 copy-done.69
  7.5 0.0 copy-done.72
  7.5 168.4 %shard_map.122 = (f32[1,512]{1,0:T(1,128)}, f32[1,512]{1,0:T(1,128)}, f32[1,128]{1,0:T(1,128)}) custom-call(s32[128]{0:T(128)S(1)} %copy-done, bf16[4,8,64,256]{3,2,1,0:T(8,128)(2,1)S(1)} %bitcast.1803, f32[1,256]{1,0:T(1,128)S(1)} %copy-done.72, f32[1,256]{1,0:T(1,128)S(1)} %copy-done.63, f32[1,2,512,256]{3,2,1,0:T(8,128)S(1)} %copy-done.19, ...), custom_call_target="tpu_custom_call" | custom-call | flops 13421772800 | bytes 5242880 | tf_op jit(solution)/shard_map/pallas_call | solution.py:977
  176.5 1.0 conditional.1
  176.8 0.7 pad_maximum_fusion
  177.5 0.6 fusion.1129
  (3 shorter events, 0.0 us)
Async XLA Ops:
  3.8 1.7 copy-start.76
  4.3 3.1 %copy-start = (s32[128]{0:T(128)S(1)}, s32[128]{0:T(128)}, u32[]{:S(2)}) copy-start(s32[128]{0:T(128)} %refs_0_.1) | copy-start | bytes 1540
  4.3 3.1 %copy-start.19 = (f32[1,2,512,256]{3,2,1,0:T(8,128)S(1)}, f32[1,2,512,256]{3,2,1,0:T(8,128)}, u32[]{:S(2)}) copy-start(f32[1,2,512,256]{3,2,1,0:T(8,128)} %refs_4_.1) | copy-start | bytes 3145732
  4.3 3.1 %copy-start.59 = (f32[1,512]{1,0:T(1,128)S(1)}, f32[1,512]{1,0:T(1,128)}, u32[]{:S(2)}) copy-start(f32[1,512]{1,0:T(1,128)} %refs_8_.1) | copy-start | bytes 6148
  4.3 3.1 %copy-start.60 = (f32[1,512]{1,0:T(1,128)S(1)}, f32[1,512]{1,0:T(1,128)}, u32[]{:S(2)}) copy-start(f32[1,512]{1,0:T(1,128)} %refs_6_.1) | copy-start | bytes 6148
  4.4 3.1 %copy-start.63 = (f32[1,256]{1,0:T(1,128)S(1)}, f32[1,256]{1,0:T(1,128)}, u32[]{:S(2)}) copy-start(f32[1,256]{1,0:T(1,128)} %refs_3_.1) | copy-start | bytes 3076
  4.4 3.1 %copy-start.66 = (f32[1,512]{1,0:T(1,128)S(1)}, f32[1,512]{1,0:T(1,128)}, u32[]{:S(2)}) copy-start(f32[1,512]{1,0:T(1,128)} %refs_7_.1) | copy-start | bytes 6148
  4.4 3.1 %copy-start.69 = (f32[1,512]{1,0:T(1,128)S(1)}, f32[1,512]{1,0:T(1,128)}, u32[]{:S(2)}) copy-start(f32[1,512]{1,0:T(1,128)} %refs_9_.1) | copy-start | bytes 6148
  4.4 3.1 %copy-start.72 = (f32[1,256]{1,0:T(1,128)S(1)}, f32[1,256]{1,0:T(1,128)}, u32[]{:S(2)}) copy-start(f32[1,256]{1,0:T(1,128)} %refs_2_.1) | copy-start | bytes 3076
